TPU v7x, 512 devices: a whole 4x4x16 slice. The times are simulated.
512 devices in a mesh: ta: 8 (over z_hi, core), ha: 4 (over y), wa: 16 (over x, z_lo).
Axes of the slice: x: 4, y: 4, z: 16 (z_hi: 4, z_lo: 4; z = z_hi * 4 + z_lo), core: 2. Of those that a mesh axis runs over, the one named last changes fastest.
Arguments:
- query: bfloat16 [8, 4, 16, 64, 1792], P('ta', 'ha', 'wa'), may hold values from -80 to 80
- keys: bfloat16 [8, 4, 16, 64, 1792], P('ta', 'ha', 'wa'), may hold values from -8 to 8
- values: bfloat16 [8, 4, 16, 64, 1792], P('ta', 'ha', 'wa'), may hold values from -6 to 6
- positions: int32 [3, 8, 4, 16, 64], P(None, 'ta', 'ha', 'wa'), may hold values from 0 to 191, as said below
- window_reach: int32 [8, 4, 16, 6], P('ta', 'ha', 'wa'), may hold values 0 or 1
Outputs:
- attended: bfloat16 [8, 4, 16, 64, 1792], P('ta', 'ha', 'wa')
Inputs may be any that keep to these rules, and one draw needn't show every extreme that they name: positions[1] is a common anchor plus the token's row in the slab, positions[2] is 64 plus the token's column in the slab; positions[0] is the same for all tokens of one latent frame and rises by 1 or 2 from one frame to the next.
All inputs are finite; a program needn't handle non-finite values. No bound on the sum of `window_reach` on one device may be relied on, other than what follows from the above.
Results may differ from a plain program's by a relative error of at most 0.0035.
The roundings to bfloat16 on the way count: a program that leaves them out, or rounds other values in their place, can miss the bound.
Values may be sent and summed in bfloat16 or wider, within the bound.
A program may use at most 64 MiB of HBM per device.

v0:
```python
import math

import jax
import jax.numpy as jnp
import numpy as np
from jax import lax
from jax.sharding import PartitionSpec as P

HD = 128
RT = 16
RH = 56
RW = 56


def extended_2(x, sides, width):
    for axis, dim in sides:
        peers, length = (lax.axis_size(axis), x.shape[dim])
        up = [(i, (i + 1) % peers) for i in range(peers - 1)]
        down = [(j, i) for i, j in up]
        last = lax.slice_in_dim(x, length - width, length, axis=dim)
        first = lax.slice_in_dim(x, 0, width, axis=dim)
        before = lax.ppermute(last, axis, up)
        after = lax.ppermute(first, axis, down)
        x = jnp.concatenate([before, x, after], axis=dim)
    return x


def pair_freqs():
    group_sizes = [RT, RH, RW]
    table = np.zeros((3, HD // 2), np.float32)
    begin = 0
    for group in range(3):
        pairs = group_sizes[group] // 2
        local = np.arange(pairs, dtype=np.float32)
        table[group, begin : begin + pairs] = np.float32(256.0) ** (
            np.float32(-2.0) * local / np.float32(group_sizes[group])
        )
        begin += pairs
    return table


def partner_table():
    index = np.arange(HD)
    table = np.zeros((HD, HD), np.float32)
    table[index, index ^ 1] = 1.0
    return table


def rotate(field, positions):
    table = jnp.asarray(np.repeat(pair_freqs(), 2, axis=1))
    signs = jnp.asarray(np.tile(np.array([-1.0, 1.0], np.float32), HD // 2))
    place = positions.astype(jnp.float32)
    angle = (
        place[0][..., None] * table[0]
        + place[1][..., None] * table[1]
        + place[2][..., None] * table[2]
    )
    cosine = jnp.cos(angle)[..., None, :]
    sine = (jnp.sin(angle) * signs)[..., None, :]
    heads = field.shape[-1] // HD
    split = field.reshape(field.shape[:-1] + (heads, HD))
    partner = jnp.dot(
        split, jnp.asarray(partner_table()).astype(jnp.bfloat16), preferred_element_type=jnp.float32
    )
    turned = split.astype(jnp.float32) * cosine + partner * sine
    return turned.reshape(field.shape).astype(jnp.bfloat16)


def reach_ok(lower, upper, place, total):
    below = (lower == 1) & (place >= 1)
    above = (upper == 1) & (place + 1 < total)
    return jnp.stack([below, jnp.ones_like(below), above], axis=-1)


def window_valid(reach, place_t, place_h, place_w, total_t, total_h, total_w):
    along_t = reach_ok(reach[..., 0], reach[..., 1], place_t, total_t)
    along_h = reach_ok(reach[..., 2], reach[..., 3], place_h, total_h)
    along_w = reach_ok(reach[..., 4], reach[..., 5], place_w, total_w)
    full = along_t[..., :, None, None] & along_h[..., None, :, None] & along_w[..., None, None, :]
    return full.reshape(full.shape[:-3] + (27,))


def body(query, keys, values, positions, window_reach):
    rot_query = rotate(query, positions)
    rot_keys = rotate(keys, positions)
    paired = jnp.concatenate([rot_keys, values], axis=-1)
    section_one = extended_2(paired, (("ta", 0),), 1)
    section_two = extended_2(section_one, (("ha", 1),), 1)
    extended = extended_2(section_two, (("wa", 2),), 1)
    width = query.shape[-1]
    heads = width // HD
    tiles = query.shape[2]
    tile = query.shape[3]
    place_t = lax.axis_index("ta")
    place_h = lax.axis_index("ha")
    place_w = lax.axis_index("wa") * tiles
    total_t = lax.axis_size("ta") * query.shape[0]
    total_h = lax.axis_size("ha") * query.shape[1]
    total_w = lax.axis_size("wa") * tiles
    scale = 1.0 / math.sqrt(HD)
    block = extended.reshape((27 * tile, 2 * width))
    key_win = block[:, :width].reshape((27 * tile, heads, HD))
    value_win = block[:, width:].reshape((27 * tile, heads, HD))
    valid = window_valid(
        window_reach[0, 0, 0], place_t, place_h, place_w + 0, total_t, total_h, total_w
    )
    allowed = jnp.repeat(valid, tile)
    query_tile = rot_query[0, 0, 0].reshape((tile, heads, HD))
    scores = (
        jnp.einsum("qhd,khd->hqk", query_tile, key_win, preferred_element_type=jnp.float32) * scale
    )
    scores = jnp.where(allowed[None, None, :], scores, -jnp.inf)
    largest = jnp.max(scores, axis=-1, keepdims=True)
    expo = jnp.exp(scores - largest)
    total = jnp.sum(expo, axis=-1, keepdims=True)
    weights = (expo / total).astype(jnp.bfloat16)
    mixed = jnp.einsum("hqk,khd->qhd", weights, value_win, preferred_element_type=jnp.float32)
    results = [mixed.astype(jnp.bfloat16).reshape((tile, width))]
    return jnp.stack(results, axis=0)[None, None]


def solution(mesh):
    in_specs = (
        P("ta", "ha", "wa", None, None),
        P("ta", "ha", "wa", None, None),
        P("ta", "ha", "wa", None, None),
        P(None, "ta", "ha", "wa", None),
        P("ta", "ha", "wa", None),
    )
    out_specs = P("ta", "ha", "wa", None, None)
    return jax.shard_map(body, mesh=mesh, in_specs=in_specs, out_specs=out_specs, check_vma=False)
```

profile of v0, /device:TPU:265, one launch (start us, length us, event | category | flops | bytes accessed | tf_op | source)
XLA Modules:
  0.0 309.0 jit_solution(8298480232230434328)
XLA Ops:
  0.0 0.7 convert_element_type.48
  0.7 1.1 reshape.583
  1.8 0.9 fusion.22
  2.7 1.0 fusion.11
  3.7 0.2 copy.14
  3.9 0.2 convert_element_type.51
  4.1 1.0 constant_dynamic-update-slice_fusion
  5.1 4.6 %collective-permute-start = (bf16[1,1,1,64,3584]{4,3,2,1,0:T(8,128)(2,1)S(1)}, bf16[1,1,1,64,3584]{4,3,2,1,0:T(8,128)(2,1)S(1)}, u32[]{:S(2)}, u32[]{:S(2)}) collective-permute-start(bf16[1,1,1,64,3584]{4,3,2,1,0:T(8,128)(2,1)S(1)} %constant_dynamic-update-slice_fusion), channel_id=1, source_target_pairs={{0,64},{64,128},{128,192},{192,256},{256,320},{320,384},{384,448},... | collective-permute-start | bytes 1376264 | tf_op jit(solution)/shard_map/ppermute | solution.py:22
  9.7 1.9 collective-permute-start.1
  11.6 5.0 %collective-permute-done = bf16[1,1,1,64,3584]{4,3,2,1,0:T(8,128)(2,1)S(1)} collective-permute-done((bf16[1,1,1,64,3584]{4,3,2,1,0:T(8,128)(2,1)S(1)}, bf16[1,1,1,64,3584]{4,3,2,1,0:T(8,128)(2,1)S(1)}, u32[]{:S(2)}, u32[]{:S(2)}) %collective-permute-start) | collective-permute-done | bytes 458784 | tf_op jit(solution)/shard_map/ppermute | solution.py:22
  16.6 21.5 %collective-permute-done.1 = bf16[1,1,1,64,3584]{4,3,2,1,0:T(8,128)(2,1)S(1)} collective-permute-done((bf16[1,1,1,64,3584]{4,3,2,1,0:T(8,128)(2,1)S(1)}, bf16[1,1,1,64,3584]{4,3,2,1,0:T(8,128)(2,1)S(1)}, u32[]{:S(2)}, u32[]{:S(2)}) %collective-permute-start.1) | collective-permute-done | bytes 458784 | tf_op jit(solution)/shard_map/ppermute | solution.py:23
  38.1 0.2 pad_maximum_fusion.2
  38.3 3.2 %collective-permute-start.2 = (bf16[3,1,1,64,3584]{4,3,2,1,0:T(8,128)(2,1)S(1)}, bf16[3,1,1,64,3584]{4,3,2,1,0:T(8,128)(2,1)S(1)}, u32[]{:S(2)}, u32[]{:S(2)}) collective-permute-start(bf16[3,1,1,64,3584]{4,3,2,1,0:T(8,128)(2,1)S(1)} %pad_maximum_fusion.2), channel_id=1, source_target_pairs={{0,16},{16,32},{32,48},{1,17},{17,33},{33,49},{2,18},{18,34},{34,5... | collective-permute-start | bytes 4128776 | tf_op jit(solution)/shard_map/ppermute | solution.py:22
  41.5 2.2 collective-permute-start.3
  43.6 27.0 %collective-permute-done.2 = bf16[3,1,1,64,3584]{4,3,2,1,0:T(8,128)(2,1)S(1)} collective-permute-done((bf16[3,1,1,64,3584]{4,3,2,1,0:T(8,128)(2,1)S(1)}, bf16[3,1,1,64,3584]{4,3,2,1,0:T(8,128)(2,1)S(1)}, u32[]{:S(2)}, u32[]{:S(2)}) %collective-permute-start.2) | collective-permute-done | bytes 1376288 | tf_op jit(solution)/shard_map/ppermute | solution.py:22
  70.7 3.2 %collective-permute-done.3 = bf16[3,1,1,64,3584]{4,3,2,1,0:T(8,128)(2,1)S(1)} collective-permute-done((bf16[3,1,1,64,3584]{4,3,2,1,0:T(8,128)(2,1)S(1)}, bf16[3,1,1,64,3584]{4,3,2,1,0:T(8,128)(2,1)S(1)}, u32[]{:S(2)}, u32[]{:S(2)}) %collective-permute-start.3) | collective-permute-done | bytes 1376288 | tf_op jit(solution)/shard_map/ppermute | solution.py:23
  73.9 2.2 pad_maximum_fusion.1
  76.1 3.2 %collective-permute-start.4 = (bf16[3,3,1,64,3584]{4,3,2,1,0:T(8,128)(2,1)}, bf16[3,3,1,64,3584]{4,3,2,1,0:T(8,128)(2,1)}, u32[]{:S(2)}, u32[]{:S(2)}) collective-permute-start(bf16[3,3,1,64,3584]{4,3,2,1,0:T(8,128)(2,1)} %pad_maximum_fusion.1), channel_id=1, source_target_pairs={{0,1},{1,2},{2,3},{3,4},{4,5},{5,6},{6,7},{7,8},{8,9},{9,10},{10,1... | collective-permute-start | bytes 12386312 | tf_op jit(solution)/shard_map/ppermute | solution.py:22
  79.3 1.3 collective-permute-start.5
  80.6 1.1 reshape.586
  81.8 0.7 fusion.33
  86.9 79.2 %collective-permute-done.4 = bf16[3,3,1,64,3584]{4,3,2,1,0:T(8,128)(2,1)} collective-permute-done((bf16[3,3,1,64,3584]{4,3,2,1,0:T(8,128)(2,1)}, bf16[3,3,1,64,3584]{4,3,2,1,0:T(8,128)(2,1)}, u32[]{:S(2)}, u32[]{:S(2)}) %collective-permute-start.4) | collective-permute-done | bytes 4128800 | tf_op jit(solution)/shard_map/ppermute | solution.py:22
  166.0 94.4 %collective-permute-done.5 = bf16[3,3,1,64,3584]{4,3,2,1,0:T(8,128)(2,1)} collective-permute-done((bf16[3,3,1,64,3584]{4,3,2,1,0:T(8,128)(2,1)}, bf16[3,3,1,64,3584]{4,3,2,1,0:T(8,128)(2,1)}, u32[]{:S(2)}, u32[]{:S(2)}) %collective-permute-start.5) | collective-permute-done | bytes 4128800 | tf_op jit(solution)/shard_map/ppermute | solution.py:23
  260.4 4.9 %pad_maximum_fusion = bf16[3,3,3,64,3584]{4,3,2,1,0:T(8,128)(2,1)S(1)} fusion(bf16[3,3,1,64,3584]{4,3,2,1,0:T(8,128)(2,1)} %collective-permute-done.5, bf16[3,1,1,64,3584]{4,3,2,1,0:T(8,128)(2,1)S(1)} %collective-permute-done.3, bf16[1,1,1,64,3584]{4,3,2,1,0:T(8,128)(2,1)} %copy-done.1, bf16[1,1,1,64,3584]{4,3,2,1,0:T(8,128)(2,1)S(1)} %constant_dynamic-update-slice_fusion, ...), kind=kLoop, calls=%fused_computation.1 | loop fusion | flops 37158912 | bytes 24772608 | tf_op jit(solution)/shard_map/concatenate | solution.py:24
  265.3 4.8 %fusion.32 = (bf16[1728,1792]{1,0:T(8,128)(2,1)}, bf16[1728,1792]{1,0:T(8,128)(2,1)}) fusion(bf16[1728,3584]{1,0:T(8,128)(2,1)S(1)} %bitcast.50), kind=kLoop, calls=%fused_computation.49 | loop fusion | bytes 24772608 | tf_op jit(solution)/shard_map/slice | solution.py:102
  270.1 9.8 %copy.24 = bf16[1728,1792]{0,1:T(8,128)(2,1)} copy(bf16[1728,1792]{1,0:T(8,128)(2,1)} %get-tuple-element.5) | data formatting | bytes 12386304
  279.9 9.8 %copy.23 = bf16[1728,1792]{0,1:T(8,128)(2,1)} copy(bf16[1728,1792]{1,0:T(8,128)(2,1)} %get-tuple-element.6) | data formatting | bytes 12386304
  289.7 6.6 %fusion.13 = f32[14,64,1728]{2,1,0:T(8,128)} fusion(bf16[1728,14,128]{0,2,1:T(8,128)(2,1)} %bitcast.51, bf16[128,128,1]{1,0,2:T(8,128)(2,1)S(1)} %copy-done.2, bf16[64,14,128]{2,1,0:T(8,128)(2,1)S(1)} %reshape.586, f32[64,128]{1,0:T(8,128)S(1)} %get-tuple-element.8, f32[64,128]{1,0:T(8,128)S(1)} %get-tuple-element.7), kind=kOutput, calls=%fused_computation.21 | convolution fusion | flops 426295296 | bytes 12713984 | tf_op jit(solution)/shard_map/qhd,khd->hqk/dot_general | solution.py:110
  296.3 4.5 %fusion.34 = f32[14,64]{1,0:T(8,128)S(1)} fusion(f32[14,64,1728]{2,1,0:T(8,128)} %fusion.13, pred[1728]{0:T(1024)(128)(4,1)S(1)} %broadcast_in_dim.13), kind=kOutput, calls=%fused_computation.51 | output fusion | flops 6194879 | bytes 6198464 | tf_op jit(solution)/shard_map/sub | solution.py:114
  300.8 7.2 %fusion.14 = bf16[64,14,128]{2,0,1:T(8,128)(2,1)S(1)} fusion(bf16[1728,14,128]{0,2,1:T(8,128)(2,1)} %bitcast.52, f32[14,64]{1,0:T(8,128)S(1)} %fusion.34, f32[14,64,1728]{2,1,0:T(8,128)} %fusion.13, pred[1728]{0:T(1024)(128)(4,1)S(1)} %broadcast_in_dim.13), kind=kOutput, calls=%fused_computation.22 | convolution fusion | flops 404220480 | bytes 12620992 | tf_op jit(solution)/shard_map/hqk,khd->qhd/dot_general | solution.py:117
  308.0 0.2 copy.20
  308.2 0.9 broadcast_in_dim_stack_reshape.3
  (17 shorter events, 0.6 us)
Async XLA Ops:
  3.9 77.9 %copy-start.3 = (s32[1,1,1,6]{3,2,1,0:T(1,128)S(1)}, s32[1,1,1,6]{3,2,1,0:T(1,128)}, u32[]{:S(2)}) copy-start(s32[1,1,1,6]{3,2,1,0:T(1,128)} %param.15) | copy-start | bytes 76
  5.1 11.5 %collective-permute-start = (bf16[1,1,1,64,3584]{4,3,2,1,0:T(8,128)(2,1)S(1)}, bf16[1,1,1,64,3584]{4,3,2,1,0:T(8,128)(2,1)S(1)}, u32[]{:S(2)}, u32[]{:S(2)}) collective-permute-start(bf16[1,1,1,64,3584]{4,3,2,1,0:T(8,128)(2,1)S(1)} %constant_dynamic-update-slice_fusion), channel_id=1, source_target_pairs={{0,64},{64,128},{128,192},{192,256},{256,320},{320,384},{384,448},... | collective-permute-start | bytes 1376264 | tf_op jit(solution)/shard_map/ppermute | solution.py:22
  9.7 28.5 %collective-permute-start.1 = (bf16[1,1,1,64,3584]{4,3,2,1,0:T(8,128)(2,1)S(1)}, bf16[1,1,1,64,3584]{4,3,2,1,0:T(8,128)(2,1)S(1)}, u32[]{:S(2)}, u32[]{:S(2)}) collective-permute-start(bf16[1,1,1,64,3584]{4,3,2,1,0:T(8,128)(2,1)S(1)} %constant_dynamic-update-slice_fusion), channel_id=1, source_target_pairs={{64,0},{128,64},{192,128},{256,192},{320,256},{384,320},{448,384},... | collective-permute-start | bytes 1376264 | tf_op jit(solution)/shard_map/ppermute | solution.py:23
  16.6 57.3 %copy-start = (bf16[1,1,1,64,3584]{4,3,2,1,0:T(8,128)(2,1)}, bf16[1,1,1,64,3584]{4,3,2,1,0:T(8,128)(2,1)S(1)}, u32[]{:S(2)}) copy-start(bf16[1,1,1,64,3584]{4,3,2,1,0:T(8,128)(2,1)S(1)} %collective-permute-done) | copy-start | bytes 1376260
  38.1 38.0 %copy-start.1 = (bf16[1,1,1,64,3584]{4,3,2,1,0:T(8,128)(2,1)}, bf16[1,1,1,64,3584]{4,3,2,1,0:T(8,128)(2,1)S(1)}, u32[]{:S(2)}) copy-start(bf16[1,1,1,64,3584]{4,3,2,1,0:T(8,128)(2,1)S(1)} %collective-permute-done.1) | copy-start | bytes 1376260
  38.3 32.4 %collective-permute-start.2 = (bf16[3,1,1,64,3584]{4,3,2,1,0:T(8,128)(2,1)S(1)}, bf16[3,1,1,64,3584]{4,3,2,1,0:T(8,128)(2,1)S(1)}, u32[]{:S(2)}, u32[]{:S(2)}) collective-permute-start(bf16[3,1,1,64,3584]{4,3,2,1,0:T(8,128)(2,1)S(1)} %pad_maximum_fusion.2), channel_id=1, source_target_pairs={{0,16},{16,32},{32,48},{1,17},{17,33},{33,49},{2,18},{18,34},{34,5... | collective-permute-start | bytes 4128776 | tf_op jit(solution)/shard_map/ppermute | solution.py:22
  41.5 32.4 %collective-permute-start.3 = (bf16[3,1,1,64,3584]{4,3,2,1,0:T(8,128)(2,1)S(1)}, bf16[3,1,1,64,3584]{4,3,2,1,0:T(8,128)(2,1)S(1)}, u32[]{:S(2)}, u32[]{:S(2)}) collective-permute-start(bf16[3,1,1,64,3584]{4,3,2,1,0:T(8,128)(2,1)S(1)} %pad_maximum_fusion.2), channel_id=1, source_target_pairs={{16,0},{32,16},{48,32},{17,1},{33,17},{49,33},{18,2},{34,18},{50,3... | collective-permute-start | bytes 4128776 | tf_op jit(solution)/shard_map/ppermute | solution.py:23
  76.1 90.0 %collective-permute-start.4 = (bf16[3,3,1,64,3584]{4,3,2,1,0:T(8,128)(2,1)}, bf16[3,3,1,64,3584]{4,3,2,1,0:T(8,128)(2,1)}, u32[]{:S(2)}, u32[]{:S(2)}) collective-permute-start(bf16[3,3,1,64,3584]{4,3,2,1,0:T(8,128)(2,1)} %pad_maximum_fusion.1), channel_id=1, source_target_pairs={{0,1},{1,2},{2,3},{3,4},{4,5},{5,6},{6,7},{7,8},{8,9},{9,10},{10,1... | collective-permute-start | bytes 12386312 | tf_op jit(solution)/shard_map/ppermute | solution.py:22
  79.3 181.1 %collective-permute-start.5 = (bf16[3,3,1,64,3584]{4,3,2,1,0:T(8,128)(2,1)}, bf16[3,3,1,64,3584]{4,3,2,1,0:T(8,128)(2,1)}, u32[]{:S(2)}, u32[]{:S(2)}) collective-permute-start(bf16[3,3,1,64,3584]{4,3,2,1,0:T(8,128)(2,1)} %pad_maximum_fusion.1), channel_id=1, source_target_pairs={{1,0},{2,1},{3,2},{4,3},{5,4},{6,5},{7,6},{8,7},{9,8},{10,9},{11,1... | collective-permute-start | bytes 12386312 | tf_op jit(solution)/shard_map/ppermute | solution.py:23
  279.9 9.8 %copy-start.2 = (bf16[128,128,1]{1,0,2:T(8,128)(2,1)S(1)}, bf16[128,128,1]{1,0,2:T(8,128)(2,1)}, u32[]{:S(2)}) copy-start(bf16[128,128,1]{1,0,2:T(8,128)(2,1)} %constant.59) | copy-start | bytes 98308
where the time goes:
time: 310 us; the launch traced here: 309 us
  waiting for transfers between devices  230 us (74%)
  local copies, waits for them, and re-layouts  29.9 us (10%)
  starting transfers between devices  16.4 us (5%)
  matrix products  14.8 us (5%)
  other arithmetic  13.6 us (4%)
  between operations  4 us (1%)
    ppermute x3, waiting for transfers between devices, extended_2(): after = lax.ppermute(first, axis, down)  119 us
    ppermute x3, waiting for transfers between devices, extended_2(): before = lax.ppermute(last, axis, up)  111 us
    unnamed x11, local copies, waits for them, and re-layouts  19.6 us
    ppermute x3, starting transfers between devices, extended_2(): before = lax.ppermute(last, axis, up)  11 us
    dot_general x1, matrix products, body(): jnp.einsum('hqk,khd->qhd', weights, value_win, preferred_element_type=jnp...  7.24 us
    concatenate x3, other arithmetic, extended_2(): x = jnp.concatenate([before, x, after], axis=dim)  7.2 us
    dot_general x1, matrix products, body(): jnp.einsum('qhd,khd->hqk', query_tile, key_win, preferred_element_type=jn...  6.61 us
  transfers between devices with their start and end apart: 6, of which 6 were waited for; matrix products, arithmetic and copies ran while one was open for 1% of the time, Pallas kernels for 0%

commit v1 on v0

v1 whole, which is shorter than its diff:
```python
import functools
import math

import jax
import jax.numpy as jnp
import numpy as np
from jax import lax
from jax.experimental import pallas as pl
from jax.experimental.pallas import tpu as pltpu
from jax.sharding import PartitionSpec as P

HD = 128
RT = 16
RH = 56
RW = 56
GROUP = 2
NEG = -1e30
SCALE2 = math.log2(math.e) / math.sqrt(HD)
F32 = jnp.float32
BF16 = jnp.bfloat16
MESH = pl.DeviceIdType.MESH

T_UP, T_DOWN, HC_UP, HC_DOWN, HP_UP, HP_DOWN, Q_UP, Q_DOWN = range(8)
S_UP, S_DOWN, S_UP2, S_DOWN2, O_UP, O_DOWN = range(8, 14)
KINDS = 14


def freq_row():
    parts = []
    for size in (RT, RH, RW):
        pairs = size // 2
        local = np.arange(pairs, dtype=np.float32)
        parts.append(np.float32(256.0) ** (np.float32(-2.0) * local / np.float32(size)))
    return np.repeat(np.concatenate(parts), 2)[None, :].astype(np.float32)


def sin_cos(x):
    n = jnp.floor(x * F32(2.0 / math.pi) + F32(0.5))
    r = x - n * F32(1.5703125)
    r = r - n * F32(4.837512969970703125e-4)
    r = r - n * F32(7.549789954891882e-8)
    z = r * r
    s = ((F32(-1.9515295891e-4) * z + F32(8.3321608736e-3)) * z - F32(1.6666654611e-1)) * z * r + r
    c = (F32(2.443315711809948e-5) * z - F32(1.388731625493765e-3)) * z + F32(4.166664568298827e-2)
    c = c * z * z - F32(0.5) * z + F32(1.0)
    quadrant = n.astype(jnp.int32) & 3
    odd = (quadrant & 1) == 1
    sine = jnp.where(odd, c, s)
    cosine = jnp.where(odd, s, c)
    sine = jnp.where(quadrant >= 2, -sine, sine)
    cosine = jnp.where((quadrant == 1) | (quadrant == 2), -cosine, cosine)
    return sine, cosine


def kernel(
    sizes, chunks, tile,
    pos_ref, reach_ref, freq_ref, q_ref, k_ref, v_ref, out_ref,
    kv, qb, pen, bias, pbuf, st, sb, oout, oin, oacc, sincos, send_sem, recv_sem, pen_sem,
):
    nt, nh, nw = sizes
    t, h, w = lax.axis_index("ta"), lax.axis_index("ha"), lax.axis_index("wa")
    width = GROUP * HD

    def at(axis, index, size, step):
        return {axis: lax.rem(index + step + size, size)}

    t_up, t_down = at("ta", t, nt, 1), at("ta", t, nt, -1)
    h_up, h_down = at("ha", h, nh, 1), at("ha", h, nh, -1)
    w_up, w_down = at("wa", w, nw, 1), at("wa", w, nw, -1)
    w_up2, w_down2 = at("wa", w, nw, 2), at("wa", w, nw, -2)

    barrier = pltpu.get_barrier_semaphore()
    near = (t_up, t_down, h_up, h_down, w_up, w_down, w_up2, w_down2)
    for other in near:
        pl.semaphore_signal(barrier, inc=1, device_id=other, device_id_type=MESH)

    def copy(kind, c):
        src, dst, to = {
            T_UP: lambda: (kv.at[c, 0, 0], kv.at[c, 0, 1], t_up),
            T_DOWN: lambda: (kv.at[c, 0, 0], kv.at[c, 0, 2], t_down),
            HC_UP: lambda: (kv.at[c, 0, 0], kv.at[c, 1, 0], h_up),
            HC_DOWN: lambda: (kv.at[c, 0, 0], kv.at[c, 2, 0], h_down),
            HP_UP: lambda: (kv.at[c, 0, pl.ds(1, 2)], kv.at[c, 1, pl.ds(1, 2)], h_up),
            HP_DOWN: lambda: (kv.at[c, 0, pl.ds(1, 2)], kv.at[c, 2, pl.ds(1, 2)], h_down),
            Q_UP: lambda: (qb.at[c, 1], qb.at[c, 0], w_up),
            Q_DOWN: lambda: (qb.at[c, 1], qb.at[c, 2], w_down),
            S_UP: lambda: (st.at[c, 1], sb.at[c, 0], w_up),
            S_DOWN: lambda: (st.at[c, 0], sb.at[c, 1], w_down),
            S_UP2: lambda: (st.at[c, 1], sb.at[c, 2], w_up2),
            S_DOWN2: lambda: (st.at[c, 0], sb.at[c, 3], w_down2),
            O_UP: lambda: (oout.at[c, 1], oin.at[c, 0], w_up),
            O_DOWN: lambda: (oout.at[c, 0], oin.at[c, 1], w_down),
        }[kind]()
        return pltpu.make_async_remote_copy(
            src_ref=src, dst_ref=dst, send_sem=send_sem.at[c, kind], recv_sem=recv_sem.at[c, kind],
            device_id=to, device_id_type=MESH,
        )

    def pen_copy(side):
        return pltpu.make_async_remote_copy(
            src_ref=pen.at[1], dst_ref=pen.at[2 * side], send_sem=pen_sem.at[0, side],
            recv_sem=pen_sem.at[1, side], device_id=(w_up, w_down)[side], device_id_type=MESH,
        )

    row = lax.broadcasted_iota(jnp.int32, (8, HD), 0)
    closed = jnp.zeros((8, HD), F32)
    for side, edge in enumerate(
        (t >= 1, t + 1 < nt, h >= 1, h + 1 < nh, w >= 1, w + 1 < nw)
    ):
        value = jnp.where((reach_ref[0, 0, 0, side] == 1) & edge, F32(0.0), F32(NEG))
        closed = jnp.where(row == side, value, closed)
    pen[1] = closed

    dim = lax.broadcasted_iota(jnp.int32, (HD, tile), 0)
    place = [pos_ref[i, 0, 0, :, :].astype(F32) for i in range(3)]
    place = jnp.where(dim < RT, place[0], jnp.where(dim < RT + RH, place[1], place[2]))
    sine, cosine = sin_cos(place.T * freq_ref[...])
    sincos[0] = sine
    sincos[1] = cosine

    pl.semaphore_wait(barrier, len(near))
    for side in range(2):
        pen_copy(side).start()

    def rotated(ref, c, g):
        a = lax.broadcasted_iota(jnp.int32, (HD, HD), 0)
        b = lax.broadcasted_iota(jnp.int32, (HD, HD), 1)
        swap = jnp.where((a ^ 1) == b, jnp.where((b & 1) == 1, F32(1.0), F32(-1.0)), F32(0.0))
        x = ref[:, pl.ds(pl.multiple_of(c * width + g * HD, HD), HD)]
        partner = jnp.dot(x, swap.astype(BF16), preferred_element_type=F32)
        return (x.astype(F32) * sincos[1] + partner * sincos[0]).astype(BF16)

    def head(g):
        return pl.ds(g * HD, HD)

    def send_own(c, carry):
        for g in range(GROUP):
            kv[c, 0, 0, 0, :, head(g)] = rotated(k_ref, c, g)
        kv[c, 0, 0, 1] = v_ref[:, pl.ds(pl.multiple_of(c * width, HD), width)]
        copy(T_UP, c).start()
        copy(T_DOWN, c).start()
        copy(HC_UP, c).start()
        copy(HC_DOWN, c).start()
        for g in range(GROUP):
            qb[c, 1, :, head(g)] = rotated(q_ref, c, g)
        copy(Q_UP, c).start()
        copy(Q_DOWN, c).start()
        return carry

    lax.fori_loop(0, chunks, send_own, 0)

    for side in range(2):
        pen_copy(side).wait_recv()
    low = lax.broadcasted_iota(jnp.int32, (8, HD), 1) < tile
    for slot in range(3):
        rows = [jnp.broadcast_to(pen[slot, pl.ds(i, 1), :], (8, HD)) for i in range(6)]
        base = (rows[5], jnp.zeros((8, HD), F32), rows[4])[slot]
        along_t = (jnp.zeros((8, HD), F32), rows[0], rows[1])
        along_h = (jnp.zeros((8, HD), F32), rows[2], rows[3])
        tiles = [base + along_h[j] + along_t[i] for j in range(3) for i in range(3)]
        tiles.append(tiles[-1])
        for u in range(5):
            bias[slot, :, pl.ds(u * HD, HD)] = jnp.where(low, tiles[2 * u], tiles[2 * u + 1])

    keys = 9 * tile

    def relay(c):
        copy(T_UP, c).wait_recv()
        copy(T_DOWN, c).wait_recv()
        copy(HP_UP, c).start()
        copy(HP_DOWN, c).start()

    def scores(c):
        for kind in (HC_UP, HC_DOWN, HP_UP, HP_DOWN, Q_UP, Q_DOWN):
            copy(kind, c).wait_recv()
        lane = lax.broadcasted_iota(jnp.int32, (tile, HD), 1)
        stats = jnp.zeros((tile, HD), F32)
        for g in range(GROUP):
            q3 = qb[c, :, :, head(g)].reshape(3 * tile, HD)
            k9 = kv[c, :, :, 0, :, head(g)].reshape(keys, HD)
            d3 = lax.dot_general(q3, k9, (((1,), (1,)), ((), ())), preferred_element_type=F32)
            for slot in range(3):
                d = d3[slot * tile:(slot + 1) * tile] + bias[slot, pl.ds(0, 1), pl.ds(0, keys)]
                m = jnp.max(d, axis=1, keepdims=True)
                p = jnp.exp2((d - m) * F32(SCALE2))
                total = jnp.sum(p, axis=1, keepdims=True)
                pbuf[lax.rem(c, 2), g, pl.ds(slot * tile, tile), :] = p
                for base in ((0,), (4, 12), (8,))[slot]:
                    stats = jnp.where(lane == base + g, m, stats)
                    stats = jnp.where(lane == base + 2 + g, total, stats)
        turned = stats.T
        st[c, 0, :, pl.ds(0, tile)] = turned[0:8]
        st[c, 1, :, pl.ds(0, tile)] = turned[8:16]
        for kind in (S_UP, S_DOWN, S_UP2, S_DOWN2):
            copy(kind, c).start()

    def mix(c):
        for kind in (S_UP, S_DOWN, S_UP2, S_DOWN2):
            copy(kind, c).wait_recv()
        left, right = st[c, 0][:, :tile], st[c, 1][:, :tile]
        from_left, from_right = sb[c, 0][:, :tile], sb[c, 1][:, :tile]
        from_left2, from_right2 = sb[c, 2][:, :tile], sb[c, 3][:, :tile]
        factors = []
        for mine, other, third in (
            (left[0:4], from_left[4:8], from_left2[0:4]),
            (left[4:8], from_left[0:4], from_right[0:4]),
            (right[0:4], from_right[4:8], from_right2[0:4]),
        ):
            ms = [x[0:2] for x in (mine, other, third)]
            ls = [x[2:4] for x in (mine, other, third)]
            top = jnp.maximum(ms[0], jnp.maximum(ms[1], ms[2]))
            es = [jnp.exp2((m - top) * F32(SCALE2)) for m in ms]
            total = es[0] * ls[0] + es[1] * ls[1] + es[2] * ls[2]
            factors.append(es[0] / total)
        factors.append(jnp.zeros((HD - 6, tile), F32))
        factor = jnp.concatenate(factors, axis=0).T
        for g in range(GROUP):
            v9 = kv[c, :, :, 1, :, head(g)].reshape(keys, HD)
            weights = []
            for slot in range(3):
                p = pbuf[lax.rem(c, 2), g, pl.ds(slot * tile, tile), :]
                weights.append((p * factor[:, 2 * slot + g:2 * slot + g + 1]).astype(BF16))
            o3 = jnp.dot(jnp.concatenate(weights, axis=0), v9, preferred_element_type=F32)
            oout[c, 0, :, head(g)] = o3[:tile].astype(BF16)
            oout[c, 1, :, head(g)] = o3[2 * tile:].astype(BF16)
            oacc[c, :, head(g)] = o3[tile:2 * tile]
        copy(O_UP, c).start()
        copy(O_DOWN, c).start()

    def finish(c):
        copy(O_UP, c).wait_recv()
        copy(O_DOWN, c).wait_recv()
        total = oacc[c] + oin[c, 0].astype(F32) + oin[c, 1].astype(F32)
        out_ref[:, pl.ds(pl.multiple_of(c * width, HD), width)] = total.astype(BF16)

    def step(s, carry):
        for lag, stage in enumerate((relay, scores, mix, finish)):
            @pl.when((s >= lag) & (s < chunks + lag))
            def _():
                stage(s - lag)
        return carry

    lax.fori_loop(0, chunks + 3, step, 0)

    def drain(c, carry):
        for kind in range(KINDS):
            copy(kind, c).wait_send()
        return carry

    lax.fori_loop(0, chunks, drain, 0)
    for side in range(2):
        pen_copy(side).wait_send()


def body(sizes, query, keys, values, positions, window_reach):
    tile, width = query.shape[-2:]
    chunks = width // (GROUP * HD)
    wide = GROUP * HD
    vmem = pl.BlockSpec(memory_space=pltpu.VMEM)
    flat = [x.reshape(tile, width) for x in (query, keys, values)]
    out = pl.pallas_call(
        functools.partial(kernel, sizes, chunks, tile),
        out_shape=jax.ShapeDtypeStruct((tile, width), BF16),
        in_specs=[vmem, pl.BlockSpec(memory_space=pltpu.SMEM), vmem, vmem, vmem, vmem],
        out_specs=vmem,
        scratch_shapes=[
            pltpu.VMEM((chunks, 3, 3, 2, tile, wide), BF16),
            pltpu.VMEM((chunks, 3, tile, wide), BF16),
            pltpu.VMEM((3, 8, HD), F32),
            pltpu.VMEM((3, 8, 5 * HD), F32),
            pltpu.VMEM((2, GROUP, 3 * tile, 9 * tile), F32),
            pltpu.VMEM((chunks, 2, 8, HD), F32),
            pltpu.VMEM((chunks, 4, 8, HD), F32),
            pltpu.VMEM((chunks, 2, tile, wide), BF16),
            pltpu.VMEM((chunks, 2, tile, wide), BF16),
            pltpu.VMEM((chunks, tile, wide), F32),
            pltpu.VMEM((2, tile, HD), F32),
            pltpu.SemaphoreType.DMA((chunks, KINDS)),
            pltpu.SemaphoreType.DMA((chunks, KINDS)),
            pltpu.SemaphoreType.DMA((2, 2)),
        ],
        compiler_params=pltpu.CompilerParams(
            collective_id=0, has_side_effects=True, vmem_limit_bytes=40 * 1024 * 1024
        ),
        name="tile_attention",
    )(positions, window_reach, jnp.asarray(freq_row()), *flat)
    return out.reshape(query.shape)


def solution(mesh):
    in_specs = (
        P("ta", "ha", "wa", None, None),
        P("ta", "ha", "wa", None, None),
        P("ta", "ha", "wa", None, None),
        P(None, "ta", "ha", "wa", None),
        P("ta", "ha", "wa", None),
    )
    out_specs = P("ta", "ha", "wa", None, None)
    sizes = tuple(mesh.shape[a] for a in ("ta", "ha", "wa"))
    return jax.shard_map(
        functools.partial(body, sizes), mesh=mesh, in_specs=in_specs, out_specs=out_specs, check_vma=False
    )
```

time: 310 us -> 78.6 us (0.25)
  the two profiles are of different devices: /device:TPU:265 before, /device:TPU:24 now
where the time goes in v1:
time: 78.6 us; the launch traced here: 78.3 us
  Pallas kernels  74.1 us (94%)
  local copies, waits for them, and re-layouts  4.19 us (5%)
    pallas_call x1, Pallas kernels, body(): pl.pallas_call(functools.partial(kernel, sizes, chunks, tile), out_shape=...  74.1 us
    unnamed x13, local copies, waits for them, and re-layouts  4.19 us

profile of v1, /device:TPU:24, one launch (start us, length us, event | category | flops | bytes accessed | tf_op | source)
XLA Modules:
  0.0 78.3 jit_solution(10385497272826552799)
XLA Ops:
  0.0 0.0 copy-start.3
  0.0 0.0 copy-start.4
  0.0 0.0 copy-start.5
  0.0 0.7 copy-done.3
  0.7 0.0 copy-done.4
  0.7 0.0 copy-done.5
  0.7 0.0 copy-start
  0.7 0.9 %copy-done = bf16[1,1,1,64,1792]{4,3,2,1,0:T(8,128)(2,1)S(1)} copy-done((bf16[1,1,1,64,1792]{4,3,2,1,0:T(8,128)(2,1)S(1)}, bf16[1,1,1,64,1792]{4,3,2,1,0:T(8,128)(2,1)}, u32[]{:S(2)}) %copy-start) | copy-done | bytes 229400
  1.6 0.0 copy-start.1
  1.6 0.9 %copy-done.1 = bf16[1,1,1,64,1792]{4,3,2,1,0:T(8,128)(2,1)S(1)} copy-done((bf16[1,1,1,64,1792]{4,3,2,1,0:T(8,128)(2,1)S(1)}, bf16[1,1,1,64,1792]{4,3,2,1,0:T(8,128)(2,1)}, u32[]{:S(2)}) %copy-start.1) | copy-done | bytes 229400
  2.6 0.0 copy-start.2
  2.6 0.9 %copy-done.2 = bf16[1,1,1,64,1792]{4,3,2,1,0:T(8,128)(2,1)S(1)} copy-done((bf16[1,1,1,64,1792]{4,3,2,1,0:T(8,128)(2,1)S(1)}, bf16[1,1,1,64,1792]{4,3,2,1,0:T(8,128)(2,1)}, u32[]{:S(2)}) %copy-start.2) | copy-done | bytes 229400
  3.5 74.1 %tile_attention.1 = bf16[64,1792]{1,0:T(8,128)(2,1)S(1)} custom-call(s32[3,1,1,1,64]{4,3,2,1,0:T(1,128)S(1)} %copy-done.3, s32[1,1,1,6]{3,2,1,0:T(1,128)S(1)} %copy-done.4, f32[1,128]{1,0:T(1,128)S(1)} %copy-done.5, bf16[64,1792]{1,0:T(8,128)(2,1)S(1)} %bitcast.5, bf16[64,1792]{1,0:T(8,128)(2,1)S(1)} %bitcast.6, bf16[64,1792]{1,0:T(8,128)(2,1)S(1)} %bitcast.7), custom_call_target="tpu_custom_call" | custom-call | tf_op jit(solution)/shard_map/tile_attention/pallas_call | solution.py:261
  77.7 0.7 copy.8
Async XLA Ops:
  0.0 0.7 copy-start.3
  0.0 0.7 copy-start.4
  0.0 0.7 copy-start.5
  0.7 0.9 %copy-start = (bf16[1,1,1,64,1792]{4,3,2,1,0:T(8,128)(2,1)S(1)}, bf16[1,1,1,64,1792]{4,3,2,1,0:T(8,128)(2,1)}, u32[]{:S(2)}) copy-start(bf16[1,1,1,64,1792]{4,3,2,1,0:T(8,128)(2,1)} %param.6) | copy-start | bytes 688132
  1.6 0.9 %copy-start.1 = (bf16[1,1,1,64,1792]{4,3,2,1,0:T(8,128)(2,1)S(1)}, bf16[1,1,1,64,1792]{4,3,2,1,0:T(8,128)(2,1)}, u32[]{:S(2)}) copy-start(bf16[1,1,1,64,1792]{4,3,2,1,0:T(8,128)(2,1)} %param.7) | copy-start | bytes 688132
  2.6 0.9 %copy-start.2 = (bf16[1,1,1,64,1792]{4,3,2,1,0:T(8,128)(2,1)S(1)}, bf16[1,1,1,64,1792]{4,3,2,1,0:T(8,128)(2,1)}, u32[]{:S(2)}) copy-start(bf16[1,1,1,64,1792]{4,3,2,1,0:T(8,128)(2,1)} %param.8) | copy-start | bytes 688132

commit v2 on v1

--- a/solution.py
+++ b/solution.py
@@ -14,6 +14,10 @@
 RH = 56
 RW = 56
 GROUP = 2
+AHEAD_K = 3
+AHEAD_Q = 2
+LAGS = (0, 2, 4, 6)
+SLOTS = LAGS[2] - LAGS[1] + 1
 NEG = -1e30
 SCALE2 = math.log2(math.e) / math.sqrt(HD)
 F32 = jnp.float32
@@ -54,25 +58,55 @@
 
 def kernel(
     sizes, chunks, tile,
-    pos_ref, reach_ref, freq_ref, q_ref, k_ref, v_ref, out_ref,
-    kv, qb, pen, bias, pbuf, st, sb, oout, oin, oacc, sincos, send_sem, recv_sem, pen_sem,
+    pos_hbm, reach_hbm, freq_hbm, q_hbm, k_hbm, v_hbm, out_ref,
+    pos_ref, reach_ref, freq_ref, q_ref, k_ref, kv, qb, pen, bias, pbuf, st, sb, oout, oin, oacc, sincos, send_sem, recv_sem, pen_sem, load_sem, v_sem,
 ):
     nt, nh, nw = sizes
     t, h, w = lax.axis_index("ta"), lax.axis_index("ha"), lax.axis_index("wa")
     width = GROUP * HD
 
-    def at(axis, index, size, step):
-        return {axis: lax.rem(index + step + size, size)}
-
-    t_up, t_down = at("ta", t, nt, 1), at("ta", t, nt, -1)
-    h_up, h_down = at("ha", h, nh, 1), at("ha", h, nh, -1)
-    w_up, w_down = at("wa", w, nw, 1), at("wa", w, nw, -1)
-    w_up2, w_down2 = at("wa", w, nw, 2), at("wa", w, nw, -2)
+    t_up, t_down = {"ta": t + 1}, {"ta": t - 1}
+    h_up, h_down = {"ha": h + 1}, {"ha": h - 1}
+    w_up, w_down, w_up2, w_down2 = {"wa": w + 1}, {"wa": w - 1}, {"wa": w + 2}, {"wa": w - 2}
+    has_t_up, has_t_down = t + 1 < nt, t >= 1
+    has_h_up, has_h_down = h + 1 < nh, h >= 1
+    has_w_up, has_w_down, has_w_up2, has_w_down2 = w + 1 < nw, w >= 1, w + 2 < nw, w >= 2
+    near = (
+        (t_up, has_t_up), (t_down, has_t_down), (h_up, has_h_up), (h_down, has_h_down),
+        (w_up, has_w_up), (w_down, has_w_down), (w_up2, has_w_up2), (w_down2, has_w_down2),
+    )
+    upward = {T_UP, HC_UP, HP_UP, Q_UP, S_UP, S_UP2, O_UP}
+    pairs = {
+        T_UP: (has_t_up, has_t_down), HC_UP: (has_h_up, has_h_down), HP_UP: (has_h_up, has_h_down),
+        Q_UP: (has_w_up, has_w_down), S_UP: (has_w_up, has_w_down), O_UP: (has_w_up, has_w_down),
+        S_UP2: (has_w_up2, has_w_down2),
+    }
 
     barrier = pltpu.get_barrier_semaphore()
-    near = (t_up, t_down, h_up, h_down, w_up, w_down, w_up2, w_down2)
-    for other in near:
-        pl.semaphore_signal(barrier, inc=1, device_id=other, device_id_type=MESH)
+    for other, there in near:
+        @pl.when(there)
+        def _():
+            pl.semaphore_signal(barrier, inc=1, device_id=other, device_id_type=MESH)
+
+    def barrier_wait():
+        count = sum(there.astype(jnp.int32) for _, there in near)
+        pl.semaphore_wait(barrier, count)
+
+    loads = [
+        pltpu.make_async_copy(src, dst, load_sem.at[i])
+        for i, (src, dst) in enumerate(
+            ((pos_hbm, pos_ref), (freq_hbm, freq_ref), (k_hbm, k_ref), (reach_hbm, reach_ref), (q_hbm, q_ref))
+        )
+    ]
+    for load in loads:
+        load.start()
+
+    def load_v(c):
+        columns = pl.ds(pl.multiple_of(c * width, HD), width)
+        return pltpu.make_async_copy(v_hbm.at[:, columns], kv.at[c, 0, 0, 1], v_sem.at[c])
+
+    for c in range(chunks):
+        load_v(c).start()
 
     def copy(kind, c):
         src, dst, to = {
@@ -96,12 +130,95 @@
             device_id=to, device_id_type=MESH,
         )
 
+    def guard(kind, receiving):
+        up, down = pairs[kind if kind in upward else kind - 1]
+        return up if (kind in upward) != receiving else down
+
+    def start(kind, c):
+        @pl.when(guard(kind, False))
+        def _():
+            copy(kind, c).start()
+
+    def await_recv(kind, c):
+        @pl.when(guard(kind, True))
+        def _():
+            copy(kind, c).wait_recv()
+
+    def await_send(kind, c):
+        @pl.when(guard(kind, False))
+        def _():
+            copy(kind, c).wait_send()
+
+    def blank(c, carry):
+        def fill(missing, ref, index, value=0.0):
+            @pl.when(missing)
+            def _():
+                ref[index] = jnp.full(ref.at[index].shape, value, ref.dtype)
+
+        fill(t < 1, kv, (c, 0, 1))
+        fill(t + 1 >= nt, kv, (c, 0, 2))
+        fill(h < 1, kv, (c, 1))
+        fill(h + 1 >= nh, kv, (c, 2))
+        for side, (one, two) in enumerate(((w < 1, w < 2), (w + 1 >= nw, w + 2 >= nw))):
+            fill(one, qb, (c, 2 * side))
+            fill(one, oin, (c, side))
+            fill(one, pen, 2 * side)
+            fill(one, sb, (c, side), NEG)
+            fill(two, sb, (c, 2 + side), NEG)
+        return carry
+
+    lax.fori_loop(0, chunks, blank, 0)
+
     def pen_copy(side):
         return pltpu.make_async_remote_copy(
             src_ref=pen.at[1], dst_ref=pen.at[2 * side], send_sem=pen_sem.at[0, side],
             recv_sem=pen_sem.at[1, side], device_id=(w_up, w_down)[side], device_id_type=MESH,
         )
 
+    loads[0].wait()
+    loads[1].wait()
+    dim = lax.broadcasted_iota(jnp.int32, (HD, tile), 0)
+    place = [pos_ref[i, 0, 0, :, :].astype(F32) for i in range(3)]
+    place = jnp.where(dim < RT, place[0], jnp.where(dim < RT + RH, place[1], place[2]))
+    sine, cosine = sin_cos(place.T * freq_ref[...])
+    sincos[0] = sine
+    sincos[1] = cosine
+
+    def rotated(ref, c, g):
+        a = lax.broadcasted_iota(jnp.int32, (HD, HD), 0)
+        b = lax.broadcasted_iota(jnp.int32, (HD, HD), 1)
+        swap = jnp.where((a ^ 1) == b, jnp.where((b & 1) == 1, F32(1.0), F32(-1.0)), F32(0.0))
+        x = ref[:, pl.ds(pl.multiple_of(c * width + g * HD, HD), HD)]
+        partner = jnp.dot(x, swap.astype(BF16), preferred_element_type=F32)
+        return (x.astype(F32) * sincos[1] + partner * sincos[0]).astype(BF16)
+
+    def head(g):
+        return pl.ds(g * HD, HD)
+
+    def turn_k(c):
+        for g in range(GROUP):
+            kv[c, 0, 0, 0, :, head(g)] = rotated(k_ref, c, g)
+        load_v(c).wait()
+
+    def send_k(c):
+        for kind in (T_UP, T_DOWN, HC_UP, HC_DOWN):
+            start(kind, c)
+
+    def send_q(c):
+        for g in range(GROUP):
+            qb[c, 1, :, head(g)] = rotated(q_ref, c, g)
+        start(Q_UP, c)
+        start(Q_DOWN, c)
+
+    loads[2].wait()
+    turn_k(0)
+    barrier_wait()
+    send_k(0)
+    for c in range(1, min(AHEAD_K, chunks)):
+        turn_k(c)
+        send_k(c)
+
+    loads[3].wait()
     row = lax.broadcasted_iota(jnp.int32, (8, HD), 0)
     closed = jnp.zeros((8, HD), F32)
     for side, edge in enumerate(
@@ -110,69 +227,55 @@
         value = jnp.where((reach_ref[0, 0, 0, side] == 1) & edge, F32(0.0), F32(NEG))
         closed = jnp.where(row == side, value, closed)
     pen[1] = closed
-
-    dim = lax.broadcasted_iota(jnp.int32, (HD, tile), 0)
-    place = [pos_ref[i, 0, 0, :, :].astype(F32) for i in range(3)]
-    place = jnp.where(dim < RT, place[0], jnp.where(dim < RT + RH, place[1], place[2]))
-    sine, cosine = sin_cos(place.T * freq_ref[...])
-    sincos[0] = sine
-    sincos[1] = cosine
-
-    pl.semaphore_wait(barrier, len(near))
     for side in range(2):
-        pen_copy(side).start()
-
-    def rotated(ref, c, g):
-        a = lax.broadcasted_iota(jnp.int32, (HD, HD), 0)
-        b = lax.broadcasted_iota(jnp.int32, (HD, HD), 1)
-        swap = jnp.where((a ^ 1) == b, jnp.where((b & 1) == 1, F32(1.0), F32(-1.0)), F32(0.0))
-        x = ref[:, pl.ds(pl.multiple_of(c * width + g * HD, HD), HD)]
-        partner = jnp.dot(x, swap.astype(BF16), preferred_element_type=F32)
-        return (x.astype(F32) * sincos[1] + partner * sincos[0]).astype(BF16)
-
-    def head(g):
-        return pl.ds(g * HD, HD)
-
-    def send_own(c, carry):
-        for g in range(GROUP):
-            kv[c, 0, 0, 0, :, head(g)] = rotated(k_ref, c, g)
-        kv[c, 0, 0, 1] = v_ref[:, pl.ds(pl.multiple_of(c * width, HD), width)]
-        copy(T_UP, c).start()
-        copy(T_DOWN, c).start()
-        copy(HC_UP, c).start()
-        copy(HC_DOWN, c).start()
-        for g in range(GROUP):
-            qb[c, 1, :, head(g)] = rotated(q_ref, c, g)
-        copy(Q_UP, c).start()
-        copy(Q_DOWN, c).start()
-        return carry
-
-    lax.fori_loop(0, chunks, send_own, 0)
-
-    for side in range(2):
-        pen_copy(side).wait_recv()
-    low = lax.broadcasted_iota(jnp.int32, (8, HD), 1) < tile
-    for slot in range(3):
-        rows = [jnp.broadcast_to(pen[slot, pl.ds(i, 1), :], (8, HD)) for i in range(6)]
-        base = (rows[5], jnp.zeros((8, HD), F32), rows[4])[slot]
-        along_t = (jnp.zeros((8, HD), F32), rows[0], rows[1])
-        along_h = (jnp.zeros((8, HD), F32), rows[2], rows[3])
-        tiles = [base + along_h[j] + along_t[i] for j in range(3) for i in range(3)]
-        tiles.append(tiles[-1])
-        for u in range(5):
-            bias[slot, :, pl.ds(u * HD, HD)] = jnp.where(low, tiles[2 * u], tiles[2 * u + 1])
+        @pl.when((has_w_up, has_w_down)[side])
+        def _():
+            pen_copy(side).start()
+    loads[4].wait()
+    for c in range(min(AHEAD_Q, chunks)):
+        send_q(c)
+
+    def make_bias():
+        for side in range(2):
+            @pl.when((has_w_down, has_w_up)[side])
+            def _():
+                pen_copy(side).wait_recv()
+
+        low = lax.broadcasted_iota(jnp.int32, (8, HD), 1) < tile
+        for slot in range(3):
+            rows = [jnp.broadcast_to(pen[slot, pl.ds(i, 1), :], (8, HD)) for i in range(6)]
+            base = (rows[5], jnp.zeros((8, HD), F32), rows[4])[slot]
+            along_t = (jnp.zeros((8, HD), F32), rows[0], rows[1])
+            along_h = (jnp.zeros((8, HD), F32), rows[2], rows[3])
+            tiles = [base + along_h[j] + along_t[i] for j in range(3) for i in range(3)]
+            tiles.append(tiles[-1])
+            for u in range(5):
+                bias[slot, :, pl.ds(u * HD, HD)] = jnp.where(low, tiles[2 * u], tiles[2 * u + 1])
 
     keys = 9 * tile
 
     def relay(c):
-        copy(T_UP, c).wait_recv()
-        copy(T_DOWN, c).wait_recv()
-        copy(HP_UP, c).start()
-        copy(HP_DOWN, c).start()
+        await_recv(T_UP, c)
+        await_recv(T_DOWN, c)
+        start(HP_UP, c)
+        start(HP_DOWN, c)
+
+        @pl.when(c + AHEAD_K < chunks)
+        def _():
+            turn_k(c + AHEAD_K)
+            send_k(c + AHEAD_K)
+
+        @pl.when(c + AHEAD_Q < chunks)
+        def _():
+            send_q(c + AHEAD_Q)
 
     def scores(c):
+        @pl.when(c == 0)
+        def _():
+            make_bias()
+
         for kind in (HC_UP, HC_DOWN, HP_UP, HP_DOWN, Q_UP, Q_DOWN):
-            copy(kind, c).wait_recv()
+            await_recv(kind, c)
         lane = lax.broadcasted_iota(jnp.int32, (tile, HD), 1)
         stats = jnp.zeros((tile, HD), F32)
         for g in range(GROUP):
@@ -184,7 +287,7 @@
                 m = jnp.max(d, axis=1, keepdims=True)
                 p = jnp.exp2((d - m) * F32(SCALE2))
                 total = jnp.sum(p, axis=1, keepdims=True)
-                pbuf[lax.rem(c, 2), g, pl.ds(slot * tile, tile), :] = p
+                pbuf[lax.rem(c, SLOTS), g, pl.ds(slot * tile, tile), :] = p
                 for base in ((0,), (4, 12), (8,))[slot]:
                     stats = jnp.where(lane == base + g, m, stats)
                     stats = jnp.where(lane == base + 2 + g, total, stats)
@@ -192,11 +295,11 @@
         st[c, 0, :, pl.ds(0, tile)] = turned[0:8]
         st[c, 1, :, pl.ds(0, tile)] = turned[8:16]
         for kind in (S_UP, S_DOWN, S_UP2, S_DOWN2):
-            copy(kind, c).start()
+            start(kind, c)
 
     def mix(c):
         for kind in (S_UP, S_DOWN, S_UP2, S_DOWN2):
-            copy(kind, c).wait_recv()
+            await_recv(kind, c)
         left, right = st[c, 0][:, :tile], st[c, 1][:, :tile]
         from_left, from_right = sb[c, 0][:, :tile], sb[c, 1][:, :tile]
         from_left2, from_right2 = sb[c, 2][:, :tile], sb[c, 3][:, :tile]
@@ -218,38 +321,40 @@
             v9 = kv[c, :, :, 1, :, head(g)].reshape(keys, HD)
             weights = []
             for slot in range(3):
-                p = pbuf[lax.rem(c, 2), g, pl.ds(slot * tile, tile), :]
+                p = pbuf[lax.rem(c, SLOTS), g, pl.ds(slot * tile, tile), :]
                 weights.append((p * factor[:, 2 * slot + g:2 * slot + g + 1]).astype(BF16))
             o3 = jnp.dot(jnp.concatenate(weights, axis=0), v9, preferred_element_type=F32)
             oout[c, 0, :, head(g)] = o3[:tile].astype(BF16)
             oout[c, 1, :, head(g)] = o3[2 * tile:].astype(BF16)
             oacc[c, :, head(g)] = o3[tile:2 * tile]
-        copy(O_UP, c).start()
-        copy(O_DOWN, c).start()
+        start(O_UP, c)
+        start(O_DOWN, c)
 
     def finish(c):
-        copy(O_UP, c).wait_recv()
-        copy(O_DOWN, c).wait_recv()
+        await_recv(O_UP, c)
+        await_recv(O_DOWN, c)
         total = oacc[c] + oin[c, 0].astype(F32) + oin[c, 1].astype(F32)
         out_ref[:, pl.ds(pl.multiple_of(c * width, HD), width)] = total.astype(BF16)
 
     def step(s, carry):
-        for lag, stage in enumerate((relay, scores, mix, finish)):
+        for lag, stage in zip(LAGS, (relay, scores, mix, finish)):
             @pl.when((s >= lag) & (s < chunks + lag))
             def _():
                 stage(s - lag)
         return carry
 
-    lax.fori_loop(0, chunks + 3, step, 0)
+    lax.fori_loop(0, chunks + LAGS[-1], step, 0)
 
     def drain(c, carry):
         for kind in range(KINDS):
-            copy(kind, c).wait_send()
+            await_send(kind, c)
         return carry
 
     lax.fori_loop(0, chunks, drain, 0)
     for side in range(2):
-        pen_copy(side).wait_send()
+        @pl.when((has_w_up, has_w_down)[side])
+        def _():
+            pen_copy(side).wait_send()
 
 
 def body(sizes, query, keys, values, positions, window_reach):
@@ -261,14 +366,19 @@
     out = pl.pallas_call(
         functools.partial(kernel, sizes, chunks, tile),
         out_shape=jax.ShapeDtypeStruct((tile, width), BF16),
-        in_specs=[vmem, pl.BlockSpec(memory_space=pltpu.SMEM), vmem, vmem, vmem, vmem],
+        in_specs=[pl.BlockSpec(memory_space=pl.ANY)] * 6,
         out_specs=vmem,
         scratch_shapes=[
+            pltpu.VMEM(positions.shape, jnp.int32),
+            pltpu.SMEM(window_reach.shape, jnp.int32),
+            pltpu.VMEM((1, HD), F32),
+            pltpu.VMEM((tile, width), BF16),
+            pltpu.VMEM((tile, width), BF16),
             pltpu.VMEM((chunks, 3, 3, 2, tile, wide), BF16),
             pltpu.VMEM((chunks, 3, tile, wide), BF16),
             pltpu.VMEM((3, 8, HD), F32),
             pltpu.VMEM((3, 8, 5 * HD), F32),
-            pltpu.VMEM((2, GROUP, 3 * tile, 9 * tile), F32),
+            pltpu.VMEM((SLOTS, GROUP, 3 * tile, 9 * tile), F32),
             pltpu.VMEM((chunks, 2, 8, HD), F32),
             pltpu.VMEM((chunks, 4, 8, HD), F32),
             pltpu.VMEM((chunks, 2, tile, wide), BF16),
@@ -278,6 +388,8 @@
             pltpu.SemaphoreType.DMA((chunks, KINDS)),
             pltpu.SemaphoreType.DMA((chunks, KINDS)),
             pltpu.SemaphoreType.DMA((2, 2)),
+            pltpu.SemaphoreType.DMA((5,)),
+            pltpu.SemaphoreType.DMA((chunks,)),
         ],
         compiler_params=pltpu.CompilerParams(
             collective_id=0, has_side_effects=True, vmem_limit_bytes=40 * 1024 * 1024

time: 78.6 us -> 60.6 us (0.77)
  the two profiles are of different devices: /device:TPU:24 before, /device:TPU:159 now
where the time goes in v2:
time: 60.6 us; the launch traced here: 60.4 us
  Pallas kernels  56.2 us (93%)
  local copies, waits for them, and re-layouts  4.19 us (7%)
    pallas_call x1, Pallas kernels, body(): pl.pallas_call(functools.partial(kernel, sizes, chunks, tile), out_shape=...  56.2 us
    unnamed x13, local copies, waits for them, and re-layouts  4.19 us

profile of v2, /device:TPU:159, one launch (start us, length us, event | category | flops | bytes accessed | tf_op | source)
XLA Modules:
  0.0 60.4 jit_solution(6623586366379322413)
XLA Ops:
  0.0 0.0 copy-start.3
  0.0 0.0 copy-start.4
  0.0 0.0 copy-start.5
  0.0 0.7 %copy-done.3 = s32[3,1,1,1,64]{4,3,2,1,0:T(1,128)S(1)} copy-done((s32[3,1,1,1,64]{4,3,2,1,0:T(1,128)S(1)}, s32[3,1,1,1,64]{4,3,2,1,0:T(1,128)}, u32[]{:S(2)}) %copy-start.3) | copy-done | bytes 792
  0.7 0.0 copy-done.4
  0.7 0.0 copy-done.5
  0.7 0.0 copy-start
  0.7 0.9 %copy-done = bf16[1,1,1,64,1792]{4,3,2,1,0:T(8,128)(2,1)S(1)} copy-done((bf16[1,1,1,64,1792]{4,3,2,1,0:T(8,128)(2,1)S(1)}, bf16[1,1,1,64,1792]{4,3,2,1,0:T(8,128)(2,1)}, u32[]{:S(2)}) %copy-start) | copy-done | bytes 229400
  1.6 0.0 copy-start.1
  1.6 0.9 %copy-done.1 = bf16[1,1,1,64,1792]{4,3,2,1,0:T(8,128)(2,1)S(1)} copy-done((bf16[1,1,1,64,1792]{4,3,2,1,0:T(8,128)(2,1)S(1)}, bf16[1,1,1,64,1792]{4,3,2,1,0:T(8,128)(2,1)}, u32[]{:S(2)}) %copy-start.1) | copy-done | bytes 229400
  2.6 0.0 copy-start.2
  2.6 0.9 %copy-done.2 = bf16[1,1,1,64,1792]{4,3,2,1,0:T(8,128)(2,1)S(1)} copy-done((bf16[1,1,1,64,1792]{4,3,2,1,0:T(8,128)(2,1)S(1)}, bf16[1,1,1,64,1792]{4,3,2,1,0:T(8,128)(2,1)}, u32[]{:S(2)}) %copy-start.2) | copy-done | bytes 229400
  3.5 56.2 %tile_attention.1 = bf16[64,1792]{1,0:T(8,128)(2,1)S(1)} custom-call(s32[3,1,1,1,64]{4,3,2,1,0:T(1,128)S(1)} %copy-done.3, s32[1,1,1,6]{3,2,1,0:T(1,128)S(1)} %copy-done.4, f32[1,128]{1,0:T(1,128)S(1)} %copy-done.5, bf16[64,1792]{1,0:T(8,128)(2,1)S(1)} %bitcast.5, bf16[64,1792]{1,0:T(8,128)(2,1)S(1)} %bitcast.6, bf16[64,1792]{1,0:T(8,128)(2,1)S(1)} %bitcast.7), custom_call_target="tpu_custom_call" | custom-call | tf_op jit(solution)/shard_map/tile_attention/pallas_call | solution.py:366
  59.7 0.7 %copy.8 = bf16[1,1,1,64,1792]{4,3,2,1,0:T(8,128)(2,1)} copy(bf16[1,1,1,64,1792]{4,3,2,1,0:T(8,128)(2,1)S(1)} %bitcast.4) | data formatting | bytes 458752
Async XLA Ops:
  0.0 0.7 %copy-start.3 = (s32[3,1,1,1,64]{4,3,2,1,0:T(1,128)S(1)}, s32[3,1,1,1,64]{4,3,2,1,0:T(1,128)}, u32[]{:S(2)}) copy-start(s32[3,1,1,1,64]{4,3,2,1,0:T(1,128)} %pos_hbm.1) | copy-start | bytes 2308
  0.0 0.7 %copy-start.4 = (s32[1,1,1,6]{3,2,1,0:T(1,128)S(1)}, s32[1,1,1,6]{3,2,1,0:T(1,128)}, u32[]{:S(2)}) copy-start(s32[1,1,1,6]{3,2,1,0:T(1,128)} %reach_hbm.1) | copy-start | bytes 76
  0.0 0.7 %copy-start.5 = (f32[1,128]{1,0:T(1,128)S(1)}, f32[1,128]{1,0:T(1,128)}, u32[]{:S(2)}) copy-start(f32[1,128]{1,0:T(1,128)} %constant.2.clone.freq_hbm) | copy-start | bytes 1540
  0.7 0.9 %copy-start = (bf16[1,1,1,64,1792]{4,3,2,1,0:T(8,128)(2,1)S(1)}, bf16[1,1,1,64,1792]{4,3,2,1,0:T(8,128)(2,1)}, u32[]{:S(2)}) copy-start(bf16[1,1,1,64,1792]{4,3,2,1,0:T(8,128)(2,1)} %param.6) | copy-start | bytes 688132
  1.6 0.9 %copy-start.1 = (bf16[1,1,1,64,1792]{4,3,2,1,0:T(8,128)(2,1)S(1)}, bf16[1,1,1,64,1792]{4,3,2,1,0:T(8,128)(2,1)}, u32[]{:S(2)}) copy-start(bf16[1,1,1,64,1792]{4,3,2,1,0:T(8,128)(2,1)} %param.7) | copy-start | bytes 688132
  2.6 0.9 %copy-start.2 = (bf16[1,1,1,64,1792]{4,3,2,1,0:T(8,128)(2,1)S(1)}, bf16[1,1,1,64,1792]{4,3,2,1,0:T(8,128)(2,1)}, u32[]{:S(2)}) copy-start(bf16[1,1,1,64,1792]{4,3,2,1,0:T(8,128)(2,1)} %param.8) | copy-start | bytes 688132

commit v3 on v2

--- a/solution.py
+++ b/solution.py
@@ -14,9 +14,9 @@
 RH = 56
 RW = 56
 GROUP = 2
-AHEAD_K = 3
+AHEAD_K = 4
 AHEAD_Q = 2
-LAGS = (0, 2, 4, 6)
+LAGS = (0, 2, 5, 8)
 SLOTS = LAGS[2] - LAGS[1] + 1
 NEG = -1e30
 SCALE2 = math.log2(math.e) / math.sqrt(HD)
@@ -24,9 +24,9 @@
 BF16 = jnp.bfloat16
 MESH = pl.DeviceIdType.MESH
 
-T_UP, T_DOWN, HC_UP, HC_DOWN, HP_UP, HP_DOWN, Q_UP, Q_DOWN = range(8)
-S_UP, S_DOWN, S_UP2, S_DOWN2, O_UP, O_DOWN = range(8, 14)
-KINDS = 14
+T_OUT, T_IN, HC_UP, HC_DOWN, HI_UP, HI_DOWN, HO_UP, HO_DOWN, Q_UP, Q_DOWN = range(10)
+S_UP, S_DOWN, S_UP2, S_DOWN2, O_UP, O_DOWN = range(10, 16)
+KINDS = 16
 
 
 def freq_row():
@@ -59,38 +59,48 @@
 def kernel(
     sizes, chunks, tile,
     pos_hbm, reach_hbm, freq_hbm, q_hbm, k_hbm, v_hbm, out_ref,
-    pos_ref, reach_ref, freq_ref, q_ref, k_ref, kv, qb, pen, bias, pbuf, st, sb, oout, oin, oacc, sincos, send_sem, recv_sem, pen_sem, load_sem, v_sem,
+    pos_ref, reach_ref, freq_ref, q_ref, k_ref, kv, qb, pen, bias, pbuf, st, sb, tops, oout, oin, oacc, sincos, send_sem, recv_sem, pen_sem, load_sem, v_sem, entry_sem,
 ):
     nt, nh, nw = sizes
     t, h, w = lax.axis_index("ta"), lax.axis_index("ha"), lax.axis_index("wa")
     width = GROUP * HD
 
-    t_up, t_down = {"ta": t + 1}, {"ta": t - 1}
+    odd = lax.rem(t, 2)
+    even = odd == 0
+    i_out, i_in = 1 + odd, 2 - odd
+    t_out, t_in = {"ta": t - 1 + 2 * odd}, {"ta": t + 1 - 2 * odd}
     h_up, h_down = {"ha": h + 1}, {"ha": h - 1}
     w_up, w_down, w_up2, w_down2 = {"wa": w + 1}, {"wa": w - 1}, {"wa": w + 2}, {"wa": w - 2}
-    has_t_up, has_t_down = t + 1 < nt, t >= 1
+    has_out = (t - 1 + 2 * odd >= 0) & (t - 1 + 2 * odd < nt)
+    always = t >= 0
     has_h_up, has_h_down = h + 1 < nh, h >= 1
     has_w_up, has_w_down, has_w_up2, has_w_down2 = w + 1 < nw, w >= 1, w + 2 < nw, w >= 2
-    near = (
-        (t_up, has_t_up), (t_down, has_t_down), (h_up, has_h_up), (h_down, has_h_down),
-        (w_up, has_w_up), (w_down, has_w_down), (w_up2, has_w_up2), (w_down2, has_w_down2),
+    beside = (
+        (h_up, has_h_up), (h_down, has_h_down), (w_up, has_w_up), (w_down, has_w_down),
+        (w_up2, has_w_up2), (w_down2, has_w_down2),
     )
-    upward = {T_UP, HC_UP, HP_UP, Q_UP, S_UP, S_UP2, O_UP}
+    upward = {HC_UP, HI_UP, HO_UP, Q_UP, S_UP, S_UP2, O_UP}
     pairs = {
-        T_UP: (has_t_up, has_t_down), HC_UP: (has_h_up, has_h_down), HP_UP: (has_h_up, has_h_down),
+        HC_UP: (has_h_up, has_h_down), HI_UP: (has_h_up, has_h_down),
+        HO_UP: (has_h_up & has_out, has_h_down & has_out),
         Q_UP: (has_w_up, has_w_down), S_UP: (has_w_up, has_w_down), O_UP: (has_w_up, has_w_down),
         S_UP2: (has_w_up2, has_w_down2),
     }
 
     barrier = pltpu.get_barrier_semaphore()
-    for other, there in near:
+
+    @pl.when(has_out & (odd == 1))
+    def _():
+        pl.semaphore_signal(barrier, inc=1, device_id=t_out, device_id_type=MESH)
+
+    for other, there in beside:
         @pl.when(there)
         def _():
-            pl.semaphore_signal(barrier, inc=1, device_id=other, device_id_type=MESH)
-
-    def barrier_wait():
-        count = sum(there.astype(jnp.int32) for _, there in near)
-        pl.semaphore_wait(barrier, count)
+            pl.semaphore_signal(barrier, inc=1, device_id={"ta": t + 1 - odd, **other}, device_id_type=MESH)
+
+    @pl.when(even)
+    def _():
+        pl.semaphore_signal(barrier, inc=1, device_id=t_in, device_id_type=MESH)
 
     loads = [
         pltpu.make_async_copy(src, dst, load_sem.at[i])
@@ -108,20 +118,23 @@
     for c in range(chunks):
         load_v(c).start()
 
-    def copy(kind, c):
+    def copy(kind, c, landing=False):
+        own, outer, inner = kv.at[c, 0, 0], kv.at[c, 0, i_out], kv.at[c, 0, i_in]
         src, dst, to = {
-            T_UP: lambda: (kv.at[c, 0, 0], kv.at[c, 0, 1], t_up),
-            T_DOWN: lambda: (kv.at[c, 0, 0], kv.at[c, 0, 2], t_down),
-            HC_UP: lambda: (kv.at[c, 0, 0], kv.at[c, 1, 0], h_up),
-            HC_DOWN: lambda: (kv.at[c, 0, 0], kv.at[c, 2, 0], h_down),
-            HP_UP: lambda: (kv.at[c, 0, pl.ds(1, 2)], kv.at[c, 1, pl.ds(1, 2)], h_up),
-            HP_DOWN: lambda: (kv.at[c, 0, pl.ds(1, 2)], kv.at[c, 2, pl.ds(1, 2)], h_down),
+            T_OUT: lambda: (own, outer if landing else inner, t_out),
+            T_IN: lambda: (own, inner if landing else outer, t_in),
+            HC_UP: lambda: (own, kv.at[c, 1, 0], h_up),
+            HC_DOWN: lambda: (own, kv.at[c, 2, 0], h_down),
+            HI_UP: lambda: (inner, kv.at[c, 1, i_in], h_up),
+            HI_DOWN: lambda: (inner, kv.at[c, 2, i_in], h_down),
+            HO_UP: lambda: (outer, kv.at[c, 1, i_out], h_up),
+            HO_DOWN: lambda: (outer, kv.at[c, 2, i_out], h_down),
             Q_UP: lambda: (qb.at[c, 1], qb.at[c, 0], w_up),
             Q_DOWN: lambda: (qb.at[c, 1], qb.at[c, 2], w_down),
             S_UP: lambda: (st.at[c, 1], sb.at[c, 0], w_up),
             S_DOWN: lambda: (st.at[c, 0], sb.at[c, 1], w_down),
-            S_UP2: lambda: (st.at[c, 1], sb.at[c, 2], w_up2),
-            S_DOWN2: lambda: (st.at[c, 0], sb.at[c, 3], w_down2),
+            S_UP2: lambda: (st.at[c, 1, 0], sb.at[c, 2, 0], w_up2),
+            S_DOWN2: lambda: (st.at[c, 0, 0], sb.at[c, 3, 0], w_down2),
             O_UP: lambda: (oout.at[c, 1], oin.at[c, 0], w_up),
             O_DOWN: lambda: (oout.at[c, 0], oin.at[c, 1], w_down),
         }[kind]()
@@ -131,6 +144,8 @@
         )
 
     def guard(kind, receiving):
+        if kind in (T_OUT, T_IN):
+            return has_out if kind == T_OUT else always
         up, down = pairs[kind if kind in upward else kind - 1]
         return up if (kind in upward) != receiving else down
 
@@ -142,7 +157,7 @@
     def await_recv(kind, c):
         @pl.when(guard(kind, True))
         def _():
-            copy(kind, c).wait_recv()
+            copy(kind, c, True).wait_recv()
 
     def await_send(kind, c):
         @pl.when(guard(kind, False))
@@ -155,8 +170,7 @@
             def _():
                 ref[index] = jnp.full(ref.at[index].shape, value, ref.dtype)
 
-        fill(t < 1, kv, (c, 0, 1))
-        fill(t + 1 >= nt, kv, (c, 0, 2))
+        fill(jnp.logical_not(has_out), kv, (c, slice(None), i_out))
         fill(h < 1, kv, (c, 1))
         fill(h + 1 >= nh, kv, (c, 2))
         for side, (one, two) in enumerate(((w < 1, w < 2), (w + 1 >= nw, w + 2 >= nw))):
@@ -200,10 +214,6 @@
             kv[c, 0, 0, 0, :, head(g)] = rotated(k_ref, c, g)
         load_v(c).wait()
 
-    def send_k(c):
-        for kind in (T_UP, T_DOWN, HC_UP, HC_DOWN):
-            start(kind, c)
-
     def send_q(c):
         for g in range(GROUP):
             qb[c, 1, :, head(g)] = rotated(q_ref, c, g)
@@ -212,11 +222,29 @@
 
     loads[2].wait()
     turn_k(0)
-    barrier_wait()
-    send_k(0)
+    near_sem, out_sem = entry_sem.at[0], entry_sem.at[1]
+
+    @pl.when(even & has_out)
+    def _():
+        pl.semaphore_wait(barrier, 1)
+        pl.semaphore_signal(out_sem, inc=1, device_id=t_out, device_id_type=MESH)
+        start(T_OUT, 0)
+
     for c in range(1, min(AHEAD_K, chunks)):
         turn_k(c)
-        send_k(c)
+
+        @pl.when(even & has_out)
+        def _():
+            start(T_OUT, c)
+
+    @pl.when(odd == 1)
+    def _():
+        pl.semaphore_wait(barrier, 1 + 2 * sum(there.astype(jnp.int32) for _, there in beside))
+        pl.semaphore_signal(near_sem, inc=1, device_id=t_in, device_id_type=MESH)
+
+    @pl.when(even)
+    def _():
+        pl.semaphore_wait(near_sem, 1)
 
     loads[3].wait()
     row = lax.broadcasted_iota(jnp.int32, (8, HD), 0)
@@ -232,8 +260,36 @@
         def _():
             pen_copy(side).start()
     loads[4].wait()
-    for c in range(min(AHEAD_Q, chunks)):
-        send_q(c)
+
+    def send_own(c, carry):
+        @pl.when(c >= AHEAD_K)
+        def _():
+            turn_k(c)
+
+        for kind in (T_IN, HC_UP, HC_DOWN):
+            start(kind, c)
+
+        @pl.when(c < AHEAD_Q)
+        def _():
+            send_q(c)
+
+        return carry
+
+    lax.fori_loop(0, chunks, send_own, 0)
+
+    def relay_in(c, carry):
+        await_recv(T_IN, c)
+        start(HI_UP, c)
+        start(HI_DOWN, c)
+        return carry
+
+    lax.fori_loop(0, chunks, relay_in, 0)
+
+    @pl.when((odd == 1) & has_out)
+    def _():
+        pl.semaphore_wait(out_sem, 1)
+        for c in range(min(AHEAD_K, chunks)):
+            start(T_OUT, c)
 
     def make_bias():
         for side in range(2):
@@ -255,17 +311,15 @@
     keys = 9 * tile
 
     def relay(c):
-        await_recv(T_UP, c)
-        await_recv(T_DOWN, c)
-        start(HP_UP, c)
-        start(HP_DOWN, c)
+        await_recv(T_OUT, c)
+        start(HO_UP, c)
+        start(HO_DOWN, c)
 
         @pl.when(c + AHEAD_K < chunks)
         def _():
-            turn_k(c + AHEAD_K)
-            send_k(c + AHEAD_K)
-
-        @pl.when(c + AHEAD_Q < chunks)
+            start(T_OUT, c + AHEAD_K)
+
+        @pl.when((c + AHEAD_Q < chunks))
         def _():
             send_q(c + AHEAD_Q)
 
@@ -274,55 +328,50 @@
         def _():
             make_bias()
 
-        for kind in (HC_UP, HC_DOWN, HP_UP, HP_DOWN, Q_UP, Q_DOWN):
+        for kind in (HC_UP, HC_DOWN, HI_UP, HI_DOWN, HO_UP, HO_DOWN, Q_UP, Q_DOWN):
             await_recv(kind, c)
         lane = lax.broadcasted_iota(jnp.int32, (tile, HD), 1)
-        stats = jnp.zeros((tile, HD), F32)
+        stats = []
         for g in range(GROUP):
             q3 = qb[c, :, :, head(g)].reshape(3 * tile, HD)
             k9 = kv[c, :, :, 0, :, head(g)].reshape(keys, HD)
             d3 = lax.dot_general(q3, k9, (((1,), (1,)), ((), ())), preferred_element_type=F32)
+            columns = jnp.zeros((tile, HD), F32)
             for slot in range(3):
                 d = d3[slot * tile:(slot + 1) * tile] + bias[slot, pl.ds(0, 1), pl.ds(0, keys)]
                 m = jnp.max(d, axis=1, keepdims=True)
                 p = jnp.exp2((d - m) * F32(SCALE2))
                 total = jnp.sum(p, axis=1, keepdims=True)
                 pbuf[lax.rem(c, SLOTS), g, pl.ds(slot * tile, tile), :] = p
-                for base in ((0,), (4, 12), (8,))[slot]:
-                    stats = jnp.where(lane == base + g, m, stats)
-                    stats = jnp.where(lane == base + 2 + g, total, stats)
-        turned = stats.T
-        st[c, 0, :, pl.ds(0, tile)] = turned[0:8]
-        st[c, 1, :, pl.ds(0, tile)] = turned[8:16]
+                columns = jnp.where(lane == slot, m * F32(SCALE2) + jnp.log2(total), columns)
+                columns = jnp.where(lane == 3 + slot, m * F32(SCALE2), columns)
+            stats.append(columns)
+        rows = jnp.concatenate(stats, axis=0).T
+        st[c, 0, 0] = rows[0:1]
+        st[c, 0, 1] = rows[1:2]
+        st[c, 1, 0] = rows[2:3]
+        st[c, 1, 1] = rows[1:2]
+        tops[lax.rem(c, SLOTS)] = rows[3:6]
         for kind in (S_UP, S_DOWN, S_UP2, S_DOWN2):
             start(kind, c)
 
     def mix(c):
         for kind in (S_UP, S_DOWN, S_UP2, S_DOWN2):
             await_recv(kind, c)
-        left, right = st[c, 0][:, :tile], st[c, 1][:, :tile]
-        from_left, from_right = sb[c, 0][:, :tile], sb[c, 1][:, :tile]
-        from_left2, from_right2 = sb[c, 2][:, :tile], sb[c, 3][:, :tile]
-        factors = []
-        for mine, other, third in (
-            (left[0:4], from_left[4:8], from_left2[0:4]),
-            (left[4:8], from_left[0:4], from_right[0:4]),
-            (right[0:4], from_right[4:8], from_right2[0:4]),
-        ):
-            ms = [x[0:2] for x in (mine, other, third)]
-            ls = [x[2:4] for x in (mine, other, third)]
-            top = jnp.maximum(ms[0], jnp.maximum(ms[1], ms[2]))
-            es = [jnp.exp2((m - top) * F32(SCALE2)) for m in ms]
-            total = es[0] * ls[0] + es[1] * ls[1] + es[2] * ls[2]
-            factors.append(es[0] / total)
-        factors.append(jnp.zeros((HD - 6, tile), F32))
-        factor = jnp.concatenate(factors, axis=0).T
+        mine = (st[c, 0, 0], st[c, 0, 1], st[c, 1, 0])
+        near = (sb[c, 0, 1], sb[c, 0, 0], sb[c, 1, 1])
+        far = (sb[c, 2, 0], sb[c, 1, 0], sb[c, 3, 0])
+        mine, near, far = [jnp.concatenate(x, axis=0) for x in (mine, near, far)]
+        top = jnp.maximum(mine, jnp.maximum(near, far))
+        whole = top + jnp.log2(jnp.exp2(mine - top) + jnp.exp2(near - top) + jnp.exp2(far - top))
+        rows = jnp.exp2(tops[lax.rem(c, SLOTS)] - whole)
+        factor = jnp.concatenate([rows, jnp.zeros((HD - 3, HD), F32)], axis=0).T
         for g in range(GROUP):
             v9 = kv[c, :, :, 1, :, head(g)].reshape(keys, HD)
             weights = []
             for slot in range(3):
                 p = pbuf[lax.rem(c, SLOTS), g, pl.ds(slot * tile, tile), :]
-                weights.append((p * factor[:, 2 * slot + g:2 * slot + g + 1]).astype(BF16))
+                weights.append((p * factor[g * tile:(g + 1) * tile, slot:slot + 1]).astype(BF16))
             o3 = jnp.dot(jnp.concatenate(weights, axis=0), v9, preferred_element_type=F32)
             oout[c, 0, :, head(g)] = o3[:tile].astype(BF16)
             oout[c, 1, :, head(g)] = o3[2 * tile:].astype(BF16)
@@ -379,8 +428,9 @@
             pltpu.VMEM((3, 8, HD), F32),
             pltpu.VMEM((3, 8, 5 * HD), F32),
             pltpu.VMEM((SLOTS, GROUP, 3 * tile, 9 * tile), F32),
-            pltpu.VMEM((chunks, 2, 8, HD), F32),
-            pltpu.VMEM((chunks, 4, 8, HD), F32),
+            pltpu.VMEM((chunks, 2, 2, 1, HD), F32),
+            pltpu.VMEM((chunks, 4, 2, 1, HD), F32),
+            pltpu.VMEM((SLOTS, 3, HD), F32),
             pltpu.VMEM((chunks, 2, tile, wide), BF16),
             pltpu.VMEM((chunks, 2, tile, wide), BF16),
             pltpu.VMEM((chunks, tile, wide), F32),
@@ -390,6 +440,7 @@
             pltpu.SemaphoreType.DMA((2, 2)),
             pltpu.SemaphoreType.DMA((5,)),
             pltpu.SemaphoreType.DMA((chunks,)),
+            pltpu.SemaphoreType.REGULAR((2,)),
         ],
         compiler_params=pltpu.CompilerParams(
             collective_id=0, has_side_effects=True, vmem_limit_bytes=40 * 1024 * 1024

time: 60.6 us -> 56.8 us (0.937)
  the two profiles are of different devices: /device:TPU:159 before, /device:TPU:141 now
where the time goes in v3:
time: 56.8 us; the launch traced here: 56.6 us
  Pallas kernels  52.4 us (92%)
  local copies, waits for them, and re-layouts  4.19 us (7%)
    pallas_call x1, Pallas kernels, body(): pl.pallas_call(functools.partial(kernel, sizes, chunks, tile), out_shape=...  52.4 us
    unnamed x13, local copies, waits for them, and re-layouts  4.19 us

profile of v3, /device:TPU:141, one launch (start us, length us, event | category | flops | bytes accessed | tf_op | source)
XLA Modules:
  0.0 56.6 jit_solution(10178917876304078382)
XLA Ops:
  0.0 0.0 copy-start.3
  0.0 0.0 copy-start.4
  0.0 0.0 copy-start.5
  0.0 0.7 %copy-done.3 = s32[3,1,1,1,64]{4,3,2,1,0:T(1,128)S(1)} copy-done((s32[3,1,1,1,64]{4,3,2,1,0:T(1,128)S(1)}, s32[3,1,1,1,64]{4,3,2,1,0:T(1,128)}, u32[]{:S(2)}) %copy-start.3) | copy-done | bytes 792
  0.7 0.0 copy-done.4
  0.7 0.0 copy-done.5
  0.7 0.0 copy-start
  0.7 0.9 %copy-done = bf16[1,1,1,64,1792]{4,3,2,1,0:T(8,128)(2,1)S(1)} copy-done((bf16[1,1,1,64,1792]{4,3,2,1,0:T(8,128)(2,1)S(1)}, bf16[1,1,1,64,1792]{4,3,2,1,0:T(8,128)(2,1)}, u32[]{:S(2)}) %copy-start) | copy-done | bytes 229400
  1.6 0.0 copy-start.1
  1.6 0.9 %copy-done.1 = bf16[1,1,1,64,1792]{4,3,2,1,0:T(8,128)(2,1)S(1)} copy-done((bf16[1,1,1,64,1792]{4,3,2,1,0:T(8,128)(2,1)S(1)}, bf16[1,1,1,64,1792]{4,3,2,1,0:T(8,128)(2,1)}, u32[]{:S(2)}) %copy-start.1) | copy-done | bytes 229400
  2.6 0.0 copy-start.2
  2.6 0.9 %copy-done.2 = bf16[1,1,1,64,1792]{4,3,2,1,0:T(8,128)(2,1)S(1)} copy-done((bf16[1,1,1,64,1792]{4,3,2,1,0:T(8,128)(2,1)S(1)}, bf16[1,1,1,64,1792]{4,3,2,1,0:T(8,128)(2,1)}, u32[]{:S(2)}) %copy-start.2) | copy-done | bytes 229400
  3.5 52.4 %tile_attention.1 = bf16[64,1792]{1,0:T(8,128)(2,1)S(1)} custom-call(s32[3,1,1,1,64]{4,3,2,1,0:T(1,128)S(1)} %copy-done.3, s32[1,1,1,6]{3,2,1,0:T(1,128)S(1)} %copy-done.4, f32[1,128]{1,0:T(1,128)S(1)} %copy-done.5, bf16[64,1792]{1,0:T(8,128)(2,1)S(1)} %bitcast.5, bf16[64,1792]{1,0:T(8,128)(2,1)S(1)} %bitcast.6, bf16[64,1792]{1,0:T(8,128)(2,1)S(1)} %bitcast.7), custom_call_target="tpu_custom_call" | custom-call | tf_op jit(solution)/shard_map/tile_attention/pallas_call | solution.py:415
  55.9 0.7 %copy.8 = bf16[1,1,1,64,1792]{4,3,2,1,0:T(8,128)(2,1)} copy(bf16[1,1,1,64,1792]{4,3,2,1,0:T(8,128)(2,1)S(1)} %bitcast.4) | data formatting | bytes 458752
Async XLA Ops:
  0.0 0.7 %copy-start.3 = (s32[3,1,1,1,64]{4,3,2,1,0:T(1,128)S(1)}, s32[3,1,1,1,64]{4,3,2,1,0:T(1,128)}, u32[]{:S(2)}) copy-start(s32[3,1,1,1,64]{4,3,2,1,0:T(1,128)} %pos_hbm.1) | copy-start | bytes 2308
  0.0 0.7 %copy-start.4 = (s32[1,1,1,6]{3,2,1,0:T(1,128)S(1)}, s32[1,1,1,6]{3,2,1,0:T(1,128)}, u32[]{:S(2)}) copy-start(s32[1,1,1,6]{3,2,1,0:T(1,128)} %reach_hbm.1) | copy-start | bytes 76
  0.0 0.7 %copy-start.5 = (f32[1,128]{1,0:T(1,128)S(1)}, f32[1,128]{1,0:T(1,128)}, u32[]{:S(2)}) copy-start(f32[1,128]{1,0:T(1,128)} %constant.2.clone.freq_hbm) | copy-start | bytes 1540
  0.7 0.9 %copy-start = (bf16[1,1,1,64,1792]{4,3,2,1,0:T(8,128)(2,1)S(1)}, bf16[1,1,1,64,1792]{4,3,2,1,0:T(8,128)(2,1)}, u32[]{:S(2)}) copy-start(bf16[1,1,1,64,1792]{4,3,2,1,0:T(8,128)(2,1)} %param.6) | copy-start | bytes 688132
  1.6 0.9 %copy-start.1 = (bf16[1,1,1,64,1792]{4,3,2,1,0:T(8,128)(2,1)S(1)}, bf16[1,1,1,64,1792]{4,3,2,1,0:T(8,128)(2,1)}, u32[]{:S(2)}) copy-start(bf16[1,1,1,64,1792]{4,3,2,1,0:T(8,128)(2,1)} %param.7) | copy-start | bytes 688132
  2.6 0.9 %copy-start.2 = (bf16[1,1,1,64,1792]{4,3,2,1,0:T(8,128)(2,1)S(1)}, bf16[1,1,1,64,1792]{4,3,2,1,0:T(8,128)(2,1)}, u32[]{:S(2)}) copy-start(bf16[1,1,1,64,1792]{4,3,2,1,0:T(8,128)(2,1)} %param.8) | copy-start | bytes 688132

commit v4 on v3

--- a/solution.py
+++ b/solution.py
@@ -58,8 +58,8 @@
 
 def kernel(
     sizes, chunks, tile,
-    pos_hbm, reach_hbm, freq_hbm, q_hbm, k_hbm, v_hbm, out_ref,
-    pos_ref, reach_ref, freq_ref, q_ref, k_ref, kv, qb, pen, bias, pbuf, st, sb, tops, oout, oin, oacc, sincos, send_sem, recv_sem, pen_sem, load_sem, v_sem, entry_sem,
+    pos_hbm, reach_hbm, freq_hbm, q_hbm, k_hbm, v_hbm, out_hbm,
+    pos_ref, reach_ref, freq_ref, q_ref, k_ref, kv, qb, pen, bias, pbuf, st, sb, tops, oout, oin, oacc, sincos, swap_ref, out_vm, send_sem, recv_sem, pen_sem, load_sem, k_sem, v_sem, out_sem, entry_sem,
 ):
     nt, nh, nw = sizes
     t, h, w = lax.axis_index("ta"), lax.axis_index("ha"), lax.axis_index("wa")
@@ -102,21 +102,28 @@
     def _():
         pl.semaphore_signal(barrier, inc=1, device_id=t_in, device_id_type=MESH)
 
-    loads = [
+    pos_load, freq_load, reach_load, q_load = [
         pltpu.make_async_copy(src, dst, load_sem.at[i])
         for i, (src, dst) in enumerate(
-            ((pos_hbm, pos_ref), (freq_hbm, freq_ref), (k_hbm, k_ref), (reach_hbm, reach_ref), (q_hbm, q_ref))
+            ((pos_hbm, pos_ref), (freq_hbm, freq_ref), (reach_hbm, reach_ref), (q_hbm, q_ref))
         )
     ]
-    for load in loads:
-        load.start()
+
+    def load_k(c):
+        columns = pl.ds(pl.multiple_of(c * width, HD), width)
+        return pltpu.make_async_copy(k_hbm.at[:, columns], k_ref.at[:, columns], k_sem.at[c])
 
     def load_v(c):
         columns = pl.ds(pl.multiple_of(c * width, HD), width)
         return pltpu.make_async_copy(v_hbm.at[:, columns], kv.at[c, 0, 0, 1], v_sem.at[c])
 
+    pos_load.start()
+    freq_load.start()
     for c in range(chunks):
+        load_k(c).start()
         load_v(c).start()
+    reach_load.start()
+    q_load.start()
 
     def copy(kind, c, landing=False):
         own, outer, inner = kv.at[c, 0, 0], kv.at[c, 0, i_out], kv.at[c, 0, i_in]
@@ -181,16 +188,18 @@
             fill(two, sb, (c, 2 + side), NEG)
         return carry
 
-    lax.fori_loop(0, chunks, blank, 0)
-
     def pen_copy(side):
         return pltpu.make_async_remote_copy(
             src_ref=pen.at[1], dst_ref=pen.at[2 * side], send_sem=pen_sem.at[0, side],
             recv_sem=pen_sem.at[1, side], device_id=(w_up, w_down)[side], device_id_type=MESH,
         )
 
-    loads[0].wait()
-    loads[1].wait()
+    a = lax.broadcasted_iota(jnp.int32, (HD, HD), 0)
+    b = lax.broadcasted_iota(jnp.int32, (HD, HD), 1)
+    swap = jnp.where((a ^ 1) == b, jnp.where((b & 1) == 1, F32(1.0), F32(-1.0)), F32(0.0))
+    swap_ref[...] = swap.astype(BF16)
+    pos_load.wait()
+    freq_load.wait()
     dim = lax.broadcasted_iota(jnp.int32, (HD, tile), 0)
     place = [pos_ref[i, 0, 0, :, :].astype(F32) for i in range(3)]
     place = jnp.where(dim < RT, place[0], jnp.where(dim < RT + RH, place[1], place[2]))
@@ -199,17 +208,15 @@
     sincos[1] = cosine
 
     def rotated(ref, c, g):
-        a = lax.broadcasted_iota(jnp.int32, (HD, HD), 0)
-        b = lax.broadcasted_iota(jnp.int32, (HD, HD), 1)
-        swap = jnp.where((a ^ 1) == b, jnp.where((b & 1) == 1, F32(1.0), F32(-1.0)), F32(0.0))
         x = ref[:, pl.ds(pl.multiple_of(c * width + g * HD, HD), HD)]
-        partner = jnp.dot(x, swap.astype(BF16), preferred_element_type=F32)
+        partner = jnp.dot(x, swap_ref[...], preferred_element_type=F32)
         return (x.astype(F32) * sincos[1] + partner * sincos[0]).astype(BF16)
 
     def head(g):
         return pl.ds(g * HD, HD)
 
     def turn_k(c):
+        load_k(c).wait()
         for g in range(GROUP):
             kv[c, 0, 0, 0, :, head(g)] = rotated(k_ref, c, g)
         load_v(c).wait()
@@ -220,14 +227,13 @@
         start(Q_UP, c)
         start(Q_DOWN, c)
 
-    loads[2].wait()
     turn_k(0)
-    near_sem, out_sem = entry_sem.at[0], entry_sem.at[1]
+    near_sem, far_sem = entry_sem.at[0], entry_sem.at[1]
 
     @pl.when(even & has_out)
     def _():
         pl.semaphore_wait(barrier, 1)
-        pl.semaphore_signal(out_sem, inc=1, device_id=t_out, device_id_type=MESH)
+        pl.semaphore_signal(far_sem, inc=1, device_id=t_out, device_id_type=MESH)
         start(T_OUT, 0)
 
     for c in range(1, min(AHEAD_K, chunks)):
@@ -246,7 +252,9 @@
     def _():
         pl.semaphore_wait(near_sem, 1)
 
-    loads[3].wait()
+    lax.fori_loop(0, chunks, blank, 0)
+
+    reach_load.wait()
     row = lax.broadcasted_iota(jnp.int32, (8, HD), 0)
     closed = jnp.zeros((8, HD), F32)
     for side, edge in enumerate(
@@ -259,7 +267,7 @@
         @pl.when((has_w_up, has_w_down)[side])
         def _():
             pen_copy(side).start()
-    loads[4].wait()
+    q_load.wait()
 
     def send_own(c, carry):
         @pl.when(c >= AHEAD_K)
@@ -287,7 +295,7 @@
 
     @pl.when((odd == 1) & has_out)
     def _():
-        pl.semaphore_wait(out_sem, 1)
+        pl.semaphore_wait(far_sem, 1)
         for c in range(min(AHEAD_K, chunks)):
             start(T_OUT, c)
 
@@ -319,7 +327,7 @@
         def _():
             start(T_OUT, c + AHEAD_K)
 
-        @pl.when((c + AHEAD_Q < chunks))
+        @pl.when(c + AHEAD_Q < chunks)
         def _():
             send_q(c + AHEAD_Q)
 
@@ -379,11 +387,28 @@
         start(O_UP, c)
         start(O_DOWN, c)
 
+    def store(c):
+        columns = pl.ds(pl.multiple_of(c * width, HD), width)
+        return pltpu.make_async_copy(out_vm.at[:, columns], out_hbm.at[:, columns], out_sem.at[c])
+
+    def settle(c):
+        await_send(O_UP, c)
+        await_send(O_DOWN, c)
+        store(c).wait()
+
     def finish(c):
         await_recv(O_UP, c)
         await_recv(O_DOWN, c)
         total = oacc[c] + oin[c, 0].astype(F32) + oin[c, 1].astype(F32)
-        out_ref[:, pl.ds(pl.multiple_of(c * width, HD), width)] = total.astype(BF16)
+        out_vm[:, pl.ds(pl.multiple_of(c * width, HD), width)] = total.astype(BF16)
+        store(c).start()
+        for kind in range(O_UP):
+            await_send(kind, c)
+
+        @pl.when(c >= 1)
+        def _():
+            settle(c - 1)
+
 
     def step(s, carry):
         for lag, stage in zip(LAGS, (relay, scores, mix, finish)):
@@ -394,12 +419,7 @@
 
     lax.fori_loop(0, chunks + LAGS[-1], step, 0)
 
-    def drain(c, carry):
-        for kind in range(KINDS):
-            await_send(kind, c)
-        return carry
-
-    lax.fori_loop(0, chunks, drain, 0)
+    settle(chunks - 1)
     for side in range(2):
         @pl.when((has_w_up, has_w_down)[side])
         def _():
@@ -410,13 +430,12 @@
     tile, width = query.shape[-2:]
     chunks = width // (GROUP * HD)
     wide = GROUP * HD
-    vmem = pl.BlockSpec(memory_space=pltpu.VMEM)
     flat = [x.reshape(tile, width) for x in (query, keys, values)]
     out = pl.pallas_call(
         functools.partial(kernel, sizes, chunks, tile),
         out_shape=jax.ShapeDtypeStruct((tile, width), BF16),
-        in_specs=[pl.BlockSpec(memory_space=pl.ANY)] * 6,
-        out_specs=vmem,
+        in_specs=[pl.BlockSpec(memory_space=pltpu.HBM)] * 6,
+        out_specs=pl.BlockSpec(memory_space=pltpu.HBM),
         scratch_shapes=[
             pltpu.VMEM(positions.shape, jnp.int32),
             pltpu.SMEM(window_reach.shape, jnp.int32),
@@ -435,15 +454,19 @@
             pltpu.VMEM((chunks, 2, tile, wide), BF16),
             pltpu.VMEM((chunks, tile, wide), F32),
             pltpu.VMEM((2, tile, HD), F32),
+            pltpu.VMEM((HD, HD), BF16),
+            pltpu.VMEM((tile, width), BF16),
             pltpu.SemaphoreType.DMA((chunks, KINDS)),
             pltpu.SemaphoreType.DMA((chunks, KINDS)),
             pltpu.SemaphoreType.DMA((2, 2)),
-            pltpu.SemaphoreType.DMA((5,)),
+            pltpu.SemaphoreType.DMA((4,)),
+            pltpu.SemaphoreType.DMA((chunks,)),
+            pltpu.SemaphoreType.DMA((chunks,)),
             pltpu.SemaphoreType.DMA((chunks,)),
             pltpu.SemaphoreType.REGULAR((2,)),
         ],
         compiler_params=pltpu.CompilerParams(
-            collective_id=0, has_side_effects=True, vmem_limit_bytes=40 * 1024 * 1024
+            collective_id=0, has_side_effects=True, vmem_limit_bytes=64 * 1024 * 1024
         ),
         name="tile_attention",
     )(positions, window_reach, jnp.asarray(freq_row()), *flat)

time: 56.8 us -> 54.8 us (0.965)
  the two profiles are of different devices: /device:TPU:141 before, /device:TPU:130 now
where the time goes in v4:
time: 54.8 us; the launch traced here: 54.7 us
  Pallas kernels  53 us (97%)
  local copies, waits for them, and re-layouts  1.64 us (3%)
    pallas_call x1, Pallas kernels, body(): pl.pallas_call(functools.partial(kernel, sizes, chunks, tile), out_shape=...  53 us
    unnamed x1, local copies, waits for them, and re-layouts  1.64 us

profile of v4, /device:TPU:130, one launch (start us, length us, event | category | flops | bytes accessed | tf_op | source)
XLA Modules:
  0.0 54.7 jit_solution(9920489528987770024)
XLA Ops:
  0.0 53.0 %tile_attention.1 = bf16[64,1792]{1,0:T(8,128)(2,1)} custom-call(s32[3,1,1,1,64]{4,3,2,1,0:T(1,128)} %pos_hbm.1, s32[1,1,1,6]{3,2,1,0:T(1,128)} %reach_hbm.1, f32[1,128]{1,0:T(1,128)} %constant.2.clone.freq_hbm, bf16[64,1792]{1,0:T(8,128)(2,1)} %bitcast.5, bf16[64,1792]{1,0:T(8,128)(2,1)} %bitcast.6, bf16[64,1792]{1,0:T(8,128)(2,1)} %bitcast.7), custom_call_target="tpu_custom_call" | custom-call | tf_op jit(solution)/shard_map/tile_attention/pallas_call | solution.py:434
  53.0 1.6 %copy.8 = bf16[1,1,1,64,1792]{4,3,2,1,0:T(8,128)(2,1)} copy(bf16[1,1,1,64,1792]{4,3,2,1,0:T(8,128)(2,1)} %bitcast.4) | data formatting | bytes 458752

commit v5 on v4

--- a/solution.py
+++ b/solution.py
@@ -466,7 +466,7 @@
             pltpu.SemaphoreType.REGULAR((2,)),
         ],
         compiler_params=pltpu.CompilerParams(
-            collective_id=0, has_side_effects=True, vmem_limit_bytes=64 * 1024 * 1024
+            collective_id=0, has_side_effects=True, vmem_limit_bytes=54920 * 1024
         ),
         name="tile_attention",
     )(positions, window_reach, jnp.asarray(freq_row()), *flat)

time: 54.8 us -> 54.2 us (0.989)
    unnamed x1 -> x7, local copies, waits for them, and re-layouts: 1.64 us -> 1.37 us
where the time goes in v5:
time: 54.2 us; the launch traced here: 54.1 us
  Pallas kernels  52.7 us (97%)
  local copies, waits for them, and re-layouts  1.37 us (3%)
    pallas_call x1, Pallas kernels, body(): pl.pallas_call(functools.partial(kernel, sizes, chunks, tile), out_shape=...  52.7 us
    unnamed x7, local copies, waits for them, and re-layouts  1.37 us

profile of v5, /device:TPU:130, one launch (start us, length us, event | category | flops | bytes accessed | tf_op | source)
XLA Modules:
  0.0 54.1 jit_solution(7175899731374068921)
XLA Ops:
  0.0 0.0 copy-start
  0.0 0.0 copy-start.1
  0.0 0.0 copy-start.2
  0.0 0.7 %copy-done = s32[3,1,1,1,64]{4,3,2,1,0:T(1,128)S(1)} copy-done((s32[3,1,1,1,64]{4,3,2,1,0:T(1,128)S(1)}, s32[3,1,1,1,64]{4,3,2,1,0:T(1,128)}, u32[]{:S(2)}) %copy-start) | copy-done | bytes 792
  0.7 0.0 copy-done.1
  0.7 0.0 copy-done.2
  0.7 52.7 %tile_attention.1 = bf16[64,1792]{1,0:T(8,128)(2,1)S(1)} custom-call(s32[3,1,1,1,64]{4,3,2,1,0:T(1,128)S(1)} %copy-done, s32[1,1,1,6]{3,2,1,0:T(1,128)S(1)} %copy-done.1, f32[1,128]{1,0:T(1,128)S(1)} %copy-done.2, bf16[64,1792]{1,0:T(8,128)(2,1)} %bitcast.5, bf16[64,1792]{1,0:T(8,128)(2,1)} %bitcast.6, bf16[64,1792]{1,0:T(8,128)(2,1)} %bitcast.7), custom_call_target="tpu_custom_call" | custom-call | tf_op jit(solution)/shard_map/tile_attention/pallas_call | solution.py:434
  53.4 0.7 %copy.8 = bf16[1,1,1,64,1792]{4,3,2,1,0:T(8,128)(2,1)} copy(bf16[1,1,1,64,1792]{4,3,2,1,0:T(8,128)(2,1)S(1)} %bitcast.4) | data formatting | bytes 458752
Async XLA Ops:
  0.0 0.7 %copy-start = (s32[3,1,1,1,64]{4,3,2,1,0:T(1,128)S(1)}, s32[3,1,1,1,64]{4,3,2,1,0:T(1,128)}, u32[]{:S(2)}) copy-start(s32[3,1,1,1,64]{4,3,2,1,0:T(1,128)} %pos_hbm.1) | copy-start | bytes 2308
  0.0 0.7 %copy-start.1 = (s32[1,1,1,6]{3,2,1,0:T(1,128)S(1)}, s32[1,1,1,6]{3,2,1,0:T(1,128)}, u32[]{:S(2)}) copy-start(s32[1,1,1,6]{3,2,1,0:T(1,128)} %reach_hbm.1) | copy-start | bytes 76
  0.0 0.7 %copy-start.2 = (f32[1,128]{1,0:T(1,128)S(1)}, f32[1,128]{1,0:T(1,128)}, u32[]{:S(2)}) copy-start(f32[1,128]{1,0:T(1,128)} %constant.2.clone.freq_hbm) | copy-start | bytes 1540

commit v6 on v5

--- a/solution.py
+++ b/solution.py
@@ -15,6 +15,7 @@
 RW = 56
 GROUP = 2
 AHEAD_K = 4
+AHEAD_H = 4
 AHEAD_Q = 2
 LAGS = (0, 2, 5, 8)
 SLOTS = LAGS[2] - LAGS[1] + 1
@@ -274,8 +275,12 @@
         def _():
             turn_k(c)
 
-        for kind in (T_IN, HC_UP, HC_DOWN):
-            start(kind, c)
+        start(T_IN, c)
+
+        @pl.when(c < AHEAD_H)
+        def _():
+            start(HC_UP, c)
+            start(HC_DOWN, c)
 
         @pl.when(c < AHEAD_Q)
         def _():
@@ -287,8 +292,12 @@
 
     def relay_in(c, carry):
         await_recv(T_IN, c)
-        start(HI_UP, c)
-        start(HI_DOWN, c)
+
+        @pl.when(c < AHEAD_H)
+        def _():
+            start(HI_UP, c)
+            start(HI_DOWN, c)
+
         return carry
 
     lax.fori_loop(0, chunks, relay_in, 0)
@@ -330,6 +339,11 @@
         @pl.when(c + AHEAD_Q < chunks)
         def _():
             send_q(c + AHEAD_Q)
+
+        @pl.when(c + AHEAD_H < chunks)
+        def _():
+            for kind in (HC_UP, HC_DOWN, HI_UP, HI_DOWN):
+                start(kind, c + AHEAD_H)
 
     def scores(c):
         @pl.when(c == 0)

time: 54.2 us -> 53.7 us (level)
  the two profiles are of different devices: /device:TPU:130 before, /device:TPU:135 now
where the time goes in v6:
time: 53.7 us; the launch traced here: 53.5 us
  Pallas kernels  52.1 us (97%)
  local copies, waits for them, and re-layouts  1.37 us (3%)
    pallas_call x1, Pallas kernels, body(): pl.pallas_call(functools.partial(kernel, sizes, chunks, tile), out_shape=...  52.1 us
    unnamed x7, local copies, waits for them, and re-layouts  1.37 us

profile of v6, /device:TPU:135, one launch (start us, length us, event | category | flops | bytes accessed | tf_op | source)
XLA Modules:
  0.0 53.5 jit_solution(13695738537103855786)
XLA Ops:
  0.0 0.0 copy-start
  0.0 0.0 copy-start.1
  0.0 0.0 copy-start.2
  0.0 0.7 %copy-done = s32[3,1,1,1,64]{4,3,2,1,0:T(1,128)S(1)} copy-done((s32[3,1,1,1,64]{4,3,2,1,0:T(1,128)S(1)}, s32[3,1,1,1,64]{4,3,2,1,0:T(1,128)}, u32[]{:S(2)}) %copy-start) | copy-done | bytes 792
  0.7 0.0 copy-done.1
  0.7 0.0 copy-done.2
  0.7 52.1 %tile_attention.1 = bf16[64,1792]{1,0:T(8,128)(2,1)S(1)} custom-call(s32[3,1,1,1,64]{4,3,2,1,0:T(1,128)S(1)} %copy-done, s32[1,1,1,6]{3,2,1,0:T(1,128)S(1)} %copy-done.1, f32[1,128]{1,0:T(1,128)S(1)} %copy-done.2, bf16[64,1792]{1,0:T(8,128)(2,1)} %bitcast.5, bf16[64,1792]{1,0:T(8,128)(2,1)} %bitcast.6, bf16[64,1792]{1,0:T(8,128)(2,1)} %bitcast.7), custom_call_target="tpu_custom_call" | custom-call | tf_op jit(solution)/shard_map/tile_attention/pallas_call | solution.py:448
  52.8 0.7 %copy.8 = bf16[1,1,1,64,1792]{4,3,2,1,0:T(8,128)(2,1)} copy(bf16[1,1,1,64,1792]{4,3,2,1,0:T(8,128)(2,1)S(1)} %bitcast.4) | data formatting | bytes 458752
Async XLA Ops:
  0.0 0.7 %copy-start = (s32[3,1,1,1,64]{4,3,2,1,0:T(1,128)S(1)}, s32[3,1,1,1,64]{4,3,2,1,0:T(1,128)}, u32[]{:S(2)}) copy-start(s32[3,1,1,1,64]{4,3,2,1,0:T(1,128)} %pos_hbm.1) | copy-start | bytes 2308
  0.0 0.7 %copy-start.1 = (s32[1,1,1,6]{3,2,1,0:T(1,128)S(1)}, s32[1,1,1,6]{3,2,1,0:T(1,128)}, u32[]{:S(2)}) copy-start(s32[1,1,1,6]{3,2,1,0:T(1,128)} %reach_hbm.1) | copy-start | bytes 76
  0.0 0.7 %copy-start.2 = (f32[1,128]{1,0:T(1,128)S(1)}, f32[1,128]{1,0:T(1,128)}, u32[]{:S(2)}) copy-start(f32[1,128]{1,0:T(1,128)} %constant.2.clone.freq_hbm) | copy-start | bytes 1540
